TPU v7x, 512 devices: a whole 4x4x16 slice. The times are simulated.
512 devices in a mesh: ctx: 8 (over x, core), ep: 64 (over y, z).
Axes of the slice: x: 4, y: 4, z: 16, core: 2. Of those that a mesh axis runs over, the one named last changes fastest.
Arguments:
- queries: bfloat16 [256, 64, 576], P('ep'), may hold values from -32 to 32
- new_key: bfloat16 [256, 576], P('ep'), may hold values from -4 to 4
- latent_cache: bfloat16 [8, 1024, 64, 576], P('ctx', 'ep'), may hold values from -6 to 6
- page_table: int32 [256, 8, 4], P('ep', 'ctx'), may hold values from 0 to 15, as said below
- lengths: int32 [256], P('ep'), may hold values from 1 to 2048
- hidden_in: bfloat16 [256, 7168], P('ep', 'ctx'), may hold values from -6 to 6
- w_uv: bfloat16 [64, 512, 128], P('ep'), may hold values from -0.25 to 0.25
- w_out: bfloat16 [8192, 7168], P('ep', 'ctx'), may hold values from -0.0625 to 0.0625
- norm_gain: float32 [7168], P('ctx'), may hold values from 0.1 to 1.9
- routes: int32 [256, 8], P('ep'), may hold values from 0 to 15, as said below
- route_weight: float32 [256, 8], P('ep'), may hold values from 0.1 to 0.6
- w_gate: bfloat16 [7168, 32768], P('ctx', 'ep'), may hold values from -0.0625 to 0.0625
- w_up: bfloat16 [7168, 32768], P('ctx', 'ep'), may hold values from -0.0625 to 0.0625
- w_down: bfloat16 [32768, 7168], P('ep', 'ctx'), may hold values from -0.125 to 0.125
Outputs:
- attn_proj: bfloat16 [256, 7168], P('ep', 'ctx')
- layer_out: bfloat16 [256, 7168], P('ep', 'ctx')
Inputs may be any that keep to these rules, and one draw needn't show every extreme that they name: The slots that page_table gives for the requests of one index of ep on one index of ctx are distinct. `routes`: each request names 8 different experts; among the 4 requests of one index of ep every expert is named by exactly 2 of them.
All inputs are finite; a program needn't handle non-finite values.
Results may differ from a plain program's by a relative error of at most 0.013.
Values may be sent and summed in bfloat16 or wider, within the bound.
A program may use at most 64 MiB of HBM per device.

v0:
```python
import jax
import jax.numpy as jnp
from jax import lax
from jax.sharding import PartitionSpec as P

D = 7168
TOP = 8
EXPERTS = 16


score_scale = 192.0 ** (-0.5)
epsilon = 1e-06
very_low = -1e30


def per_device(
    queries,
    new_key,
    latent_cache,
    page_table,
    lengths,
    hidden_in,
    w_uv,
    w_out,
    norm_gain,
    routes,
    route_weight,
    w_gate,
    w_up,
    w_down,
):
    row_count = queries.shape[0]
    ctx_count = lax.axis_size("ctx")
    ep_count = lax.axis_size("ep")
    ctx_rank = lax.axis_index("ctx")
    page_count = page_table.shape[2]
    page_len = latent_cache.shape[2]
    lat_width = w_uv.shape[1]
    slot_ids = page_table[:, 0, :]
    key_rows = latent_cache[0][slot_ids].reshape(row_count, page_count * page_len, -1)
    page_pos = (jnp.arange(page_count, dtype=jnp.int32) * ctx_count + ctx_rank) * page_len
    positions = (page_pos[:, None] + jnp.arange(page_len, dtype=jnp.int32)[None, :]).reshape(-1)
    usable = positions[None, :] < lengths[:, None]
    scores = (
        jnp.einsum("rhk,rtk->rht", queries, key_rows, preferred_element_type=jnp.float32)
        * score_scale
    )
    scores = jnp.where(usable[:, None, :], scores, very_low)
    own_score = (
        jnp.einsum("rhk,rk->rh", queries, new_key, preferred_element_type=jnp.float32) * score_scale
    )
    holds_new = (lengths // page_len % ctx_count == ctx_rank)[:, None]
    own_score = jnp.where(holds_new, own_score, very_low)
    peak_score = jnp.maximum(jnp.max(scores, axis=2), own_score)
    weights = jnp.where(usable[:, None, :], jnp.exp(scores - peak_score[..., None]), 0.0)
    own_weight = jnp.where(holds_new, jnp.exp(own_score - peak_score), 0.0)
    totals = jnp.sum(weights, axis=2) + own_weight
    latent32 = key_rows[..., :lat_width].astype(jnp.float32)
    mixture = jnp.einsum("rht,rtl->rhl", weights, latent32, precision=lax.Precision.HIGHEST)
    mixture = mixture + own_weight[..., None] * new_key[:, None, :lat_width].astype(jnp.float32)
    top_all = lax.pmax(peak_score, "ctx")
    factor = jnp.exp(peak_score - top_all)
    totals, mixture = lax.psum((totals * factor, mixture * factor[..., None]), "ctx")
    attended = (mixture / totals[..., None]).astype(jnp.bfloat16)
    gathered = lax.all_to_all(attended, "ep", split_axis=1, concat_axis=0, tiled=True)
    values = jnp.einsum("rhl,hlv->rhv", gathered, w_uv, preferred_element_type=jnp.float32).astype(
        jnp.bfloat16
    )
    values = values.reshape(values.shape[0], -1)
    attention = lax.psum_scatter(
        jnp.dot(values, w_out, preferred_element_type=jnp.float32),
        "ep",
        scatter_dimension=0,
        tiled=True,
    )
    residual = hidden_in.astype(jnp.float32) + attention
    squares = lax.psum(jnp.sum(residual * residual, axis=1), "ctx")
    normed = (residual * lax.rsqrt(squares[:, None] / D + epsilon) * norm_gain[None, :]).astype(
        jnp.bfloat16
    )
    members = ep_count // EXPERTS
    capacity = row_count * TOP // EXPERTS
    expert_ids = jnp.arange(EXPERTS, dtype=jnp.int32)
    matches = routes[:, :, None] == expert_ids[None, None, :]
    named_by = jnp.any(matches, axis=1).astype(jnp.int32)
    row_weight = jnp.sum(jnp.where(matches, route_weight[:, :, None], 0.0), axis=1)
    slot_order = jnp.cumsum(named_by, axis=0) - named_by
    slot_hit = (named_by[None, :, :] == 1) & (
        slot_order[None, :, :] == jnp.arange(capacity, dtype=jnp.int32)[:, None, None]
    )
    picker = jnp.transpose(slot_hit, (2, 0, 1))
    outgoing = jnp.einsum(
        "esr,rd->esd", picker.astype(jnp.bfloat16), normed, preferred_element_type=jnp.float32
    ).astype(jnp.bfloat16)
    outgoing = jnp.broadcast_to(
        outgoing[:, None], (EXPERTS, members, capacity, outgoing.shape[2])
    ).reshape(ep_count * capacity, -1)
    arrived = lax.all_to_all(outgoing, "ep", split_axis=0, concat_axis=0, tiled=True)
    gate_part = jnp.dot(arrived, w_gate, preferred_element_type=jnp.float32)
    up_part = jnp.dot(arrived, w_up, preferred_element_type=jnp.float32)
    gate_full, up_full = (
        lax.psum(gate_part.astype(jnp.bfloat16), "ctx").astype(jnp.float32),
        lax.psum(up_part.astype(jnp.bfloat16), "ctx").astype(jnp.float32),
    )
    middle = (jax.nn.silu(gate_full) * up_full).astype(jnp.bfloat16)
    produced = jnp.dot(middle, w_down, preferred_element_type=jnp.float32)
    returned = lax.all_to_all(
        produced.astype(jnp.bfloat16), "ep", split_axis=0, concat_axis=0, tiled=True
    ).astype(produced.dtype)
    summed = returned.reshape(EXPERTS, members, capacity, -1).sum(axis=1)
    combiner = picker.astype(jnp.float32) * jnp.transpose(row_weight)[:, None, :]
    routed = jnp.einsum("esr,esd->rd", combiner, summed, precision=lax.Precision.HIGHEST)
    return (attention.astype(jnp.bfloat16), (residual + routed).astype(jnp.bfloat16))


def solution(mesh):
    placed = (
        P("ep", None, None),
        P("ep", None),
        P("ctx", "ep", None, None),
        P("ep", "ctx", None),
        P("ep"),
        P("ep", "ctx"),
        P("ep", None, None),
        P("ep", "ctx"),
        P("ctx"),
        P("ep", None),
        P("ep", None),
        P("ctx", "ep"),
        P("ctx", "ep"),
        P("ep", "ctx"),
    )
    return jax.shard_map(
        per_device,
        mesh=mesh,
        in_specs=placed,
        out_specs=(P("ep", "ctx"), P("ep", "ctx")),
        check_vma=False,
    )
```

profile of v0, /device:TPU:6, one launch (start us, length us, event | category | flops | bytes accessed | tf_op | source)
XLA Modules:
  0.0 564.0 jit_solution(7088498654789850095)
XLA Ops:
  7.2 0.0 copy-start
  7.2 0.0 all-reduce.6.cloned.1.call-start
  7.2 0.1 iota_add_fusion
  7.3 0.1 add.84
  7.4 0.8 fusion.39
  8.2 0.7 broadcast_compare_fusion
  8.9 0.7 compare_select_fusion
  9.6 0.1 reshape.136
  9.7 0.7 slice_convert_fusion
  10.4 0.0 copy-done
  10.4 0.8 gather_fusion
  11.2 0.2 copy-done.3
  11.4 0.0 copy-done.9
  11.4 0.2 fusion.22
  11.6 0.6 fusion.44
  12.2 0.1 fusion.38
  12.3 14.3 %pmax.7 = f32[4,64]{1,0:T(4,128)S(1)} all-reduce(f32[4,64]{1,0:T(4,128)S(1)} %fusion.38), channel_id=1, replica_groups=mesh['ctx'=8,'ep'=64] {'ctx'}, use_global_device_ids=true, to_apply=%region_1.2 | all-reduce | flops 256 | bytes 2048 | tf_op jit(solution)/shard_map/pmax | solution.py:61
  26.6 0.2 fusion.12
  26.8 0.1 add_multiply_fusion
  26.8 1.5 fusion
  28.4 0.0 all-reduce.6.cloned.1.call-update
  28.4 0.0 copy-start.4
  28.4 0.0 copy-start.5
  28.4 0.0 all-reduce.8.cloned.1.call-start
  28.5 12.6 %psum.36 = f32[4,64]{1,0:T(4,128)S(1)} all-reduce(f32[4,64]{1,0:T(4,128)S(1)} %get-tuple-element.4), channel_id=1, replica_groups=mesh['ctx'=8,'ep'=64] {'ctx'}, use_global_device_ids=true, to_apply=%region_4.5 | all-reduce | flops 256 | bytes 2048 | tf_op jit(solution)/shard_map/psum | solution.py:63
  41.0 63.6 %all-reduce.6.cloned.1.call-done = f32[4,64,512]{2,1,0:T(8,128)} async-done(((f32[4,64,512]{2,1,0:T(8,128)}), f32[4,64,512]{2,1,0:T(8,128)}) %all-reduce.6.cloned.1.call-update) | async-done | bytes 524304 | tf_op jit(solution)/shard_map/psum | solution.py:63
  104.6 1.1 divide_convert_fusion
  105.8 0.2 copy.26
  106.0 37.3 %all_to_all.36 = bf16[4,64,512]{2,0,1:T(4,128)(2,1)S(1)} all-to-all(bf16[4,64,512]{2,0,1:T(4,128)(2,1)S(1)} %copy.26), channel_id=1, replica_groups=mesh['ctx'=8,'ep'=64] {'ep'}, dimensions={1} | all-to-all | bytes 524288 | tf_op jit(solution)/shard_map/all_to_all | solution.py:65
  143.3 0.1 reshape.131
  143.4 0.0 copy-done.4
  143.4 0.0 copy-done.5
  143.4 0.0 copy-start.7
  143.4 0.0 copy-start.6
  143.4 0.0 copy-start.8
  143.5 1.4 fusion.3
  144.9 0.0 all-reduce.8.cloned.1.call-update
  144.9 0.0 all-reduce.10.cloned.1.call-start
  144.9 1.3 dynamic-slice
  146.9 0.0 copy-done.7
  146.9 0.1 fusion.21
  147.1 261.0 %all-reduce.8.cloned.1.call-done = f32[256,896]{1,0:T(8,128)} async-done(((f32[256,896]{1,0:T(8,128)}), f32[256,896]{1,0:T(8,128)}) %all-reduce.8.cloned.1.call-update) | async-done | bytes 917520
  408.1 0.0 copy-done.6
  408.1 0.9 multiply_reduce_fusion
  409.0 10.0 %psum.37 = f32[4]{0:T(128)S(1)} all-reduce(f32[4]{0:T(128)S(1)} %multiply_reduce_fusion), channel_id=1, replica_groups=mesh['ctx'=8,'ep'=64] {'ctx'}, use_global_device_ids=true, to_apply=%region_10.11 | all-reduce | flops 4 | bytes 32 | tf_op jit(solution)/shard_map/psum | solution.py:77
  419.0 0.0 copy-done.8
  419.0 1.0 convolution_convert_fusion.4
  420.0 0.0 copy-start.2
  420.0 0.1 broadcast_in_dim.86
  420.2 28.4 %all_to_all.37 = bf16[64,2,896]{2,1,0:T(2,128)(2,1)} all-to-all(bf16[64,2,896]{2,1,0:T(2,128)(2,1)S(1)} %bitcast.52), channel_id=1, replica_groups=mesh['ctx'=8,'ep'=64] {'ep'}, dimensions={0} | all-to-all | bytes 458752 | tf_op jit(solution)/shard_map/all_to_all | solution.py:98
  448.6 1.0 all_to_all.30
  449.6 0.0 copy-done.1
  449.6 1.0 convolution_convert_fusion.1
  450.6 1.0 convolution_convert_fusion.2
  451.6 0.0 all-reduce.10.cloned.1.call-update
  451.6 65.5 %all-reduce.10.cloned.1.call-done = (bf16[128,512]{1,0:T(8,128)(2,1)}, bf16[128,512]{1,0:T(8,128)(2,1)}) async-done(((bf16[128,512]{1,0:T(8,128)(2,1)}, bf16[128,512]{1,0:T(8,128)(2,1)}), (bf16[128,512]{1,0:T(8,128)(2,1)}, bf16[128,512]{1,0:T(8,128)(2,1)})) %all-reduce.10.cloned.1.call-update) | async-done | bytes 262160 | tf_op jit(solution)/shard_map/psum | solution.py:103
  517.0 1.6 convolution_convert_fusion
  518.7 0.8 all_to_all.31
  519.5 15.6 %all-to-all-start.2 = ((bf16[64,2,896]{2,1,0:T(2,128)(2,1)}), bf16[64,2,896]{2,1,0:T(2,128)(2,1)S(1)}, u32[]{:S(2)}, u32[]{:S(2)}) async-start(bf16[64,2,896]{2,1,0:T(2,128)(2,1)} %all_to_all.31), calls=%async_computation.2 | async-start | bytes 458752 | tf_op jit(solution)/shard_map/all_to_all | solution.py:107
  535.1 0.1 select_reduce_fusion
  535.2 1.3 dynamic-slice_convert_fusion
  536.6 19.0 %all-to-all-done.2 = bf16[64,2,896]{2,1,0:T(2,128)(2,1)S(1)} async-done(((bf16[64,2,896]{2,1,0:T(2,128)(2,1)}), bf16[64,2,896]{2,1,0:T(2,128)(2,1)S(1)}, u32[]{:S(2)}, u32[]{:S(2)}) %all-to-all-start.2) | async-done | bytes 229408 | tf_op jit(solution)/shard_map/all_to_all | solution.py:107
  555.6 0.2 convert_reduce_fusion
  555.8 1.6 fusion.5
  (13 shorter events, 0.1 us)
Async XLA Ops:
  7.2 3.2 copy-start
  7.2 97.5 %all-reduce.6.cloned.1.call-start = ((), (), s32[]{:S(2)}) async-start(), calls=%async_computation.3 | async-start | bytes 1048576 | tf_op jit(solution)/shard_map/psum | solution.py:63
  10.4 1.0 copy-start.3
  10.4 1.0 copy-start.9
  28.4 115.0 %copy-start.4 = (bf16[128,896]{1,0:T(8,128)(2,1)S(1)}, bf16[128,896]{1,0:T(8,128)(2,1)}, u32[]{:S(2)}) copy-start(bf16[128,896]{1,0:T(8,128)(2,1)} %param.21) | copy-start | bytes 688132
  28.4 115.0 %copy-start.5 = (bf16[1,512,128]{2,1,0:T(8,128)(2,1)S(1)}, bf16[1,512,128]{2,1,0:T(8,128)(2,1)}, u32[]{:S(2)}) copy-start(bf16[1,512,128]{2,1,0:T(8,128)(2,1)} %param.20) | copy-start | bytes 393220
  28.4 379.7 %all-reduce.8.cloned.1.call-start = ((), (), s32[]{:S(2)}) async-start(), calls=%async_computation.4 | async-start | bytes 1835008
  143.4 3.5 copy-start.7
  143.4 264.7 %copy-start.6 = (bf16[4,896]{1,0:T(4,128)(2,1)S(1)}, bf16[4,896]{1,0:T(4,128)(2,1)}, u32[]{:S(2)}) copy-start(bf16[4,896]{1,0:T(4,128)(2,1)} %param.19) | copy-start | bytes 21508
  143.4 275.6 %copy-start.8 = (f32[896]{0:T(1024)S(1)}, f32[896]{0:T(1024)}, u32[]{:S(2)}) copy-start(f32[896]{0:T(1024)} %param.22) | copy-start | bytes 10756
  144.9 304.8 %copy-start.1 = (bf16[896,512]{1,0:T(8,128)(2,1)S(1)}, bf16[896,512]{1,0:T(8,128)(2,1)}, u32[]{:S(2)}) copy-start(bf16[896,512]{1,0:T(8,128)(2,1)} %param.26) | copy-start | bytes 2752516
  144.9 372.2 %all-reduce.10.cloned.1.call-start = ((), (), s32[]{:S(2)}) async-start(), calls=%async_computation.5 | async-start | bytes 524288 | tf_op jit(solution)/shard_map/psum | solution.py:103
  420.0 30.6 %copy-start.2 = (bf16[896,512]{1,0:T(8,128)(2,1)S(1)}, bf16[896,512]{1,0:T(8,128)(2,1)}, u32[]{:S(2)}) copy-start(bf16[896,512]{1,0:T(8,128)(2,1)} %param.25) | copy-start | bytes 2752516
  517.0 18.1 %copy-start.10 = (f32[4,8]{1,0:T(4,128)S(1)}, f32[4,8]{1,0:T(4,128)}, u32[]{:S(2)}) copy-start(f32[4,8]{1,0:T(4,128)} %param.24) | copy-start | bytes 388
  519.5 36.1 %all-to-all-start.2 = ((bf16[64,2,896]{2,1,0:T(2,128)(2,1)}), bf16[64,2,896]{2,1,0:T(2,128)(2,1)S(1)}, u32[]{:S(2)}, u32[]{:S(2)}) async-start(bf16[64,2,896]{2,1,0:T(2,128)(2,1)} %all_to_all.31), calls=%async_computation.2 | async-start | bytes 458752 | tf_op jit(solution)/shard_map/all_to_all | solution.py:107
Sparse Core Ops, SparseCore 0:
  28.5 76.0 all-reduce.5
  145.0 263.0 all-reduce.7
  451.7 65.2 all-reduce.9
where the time goes:
time: 565 us; the launch traced here: 564 us
  waiting for transfers between devices  409 us (72%)
  blocking collectives  103 us (18%)
  starting transfers between devices  15.8 us (3%)
  between operations  14.6 us (3%)
  matrix products  9.9 us (2%)
  local copies, waits for them, and re-layouts  6.12 us (1%)
  other arithmetic  5.77 us (1%)
    unnamed x4, waiting for transfers between devices  261 us
    psum x1, waiting for transfers between devices, per_device(): lax.psum(up_part.astype(jnp.bfloat16), 'ctx').astype(jnp.float32)  65.5 us
    psum x1, waiting for transfers between devices, per_device(): lax.psum((totals * factor, mixture * factor[..., None]), 'ctx')  63.6 us
    all_to_all x1, blocking collectives, per_device(): lax.all_to_all(attended, 'ep', split_axis=1, concat_axis=0, tiled=True)  37.3 us
    all_to_all x1, blocking collectives, per_device(): lax.all_to_all(outgoing, 'ep', split_axis=0, concat_axis=0, tiled=True)  28.4 us
    all_to_all x1, waiting for transfers between devices, per_device(): lax.all_to_all(produced.astype(jnp.bfloat16), 'ep', split_axis=0, concat_...  19 us
    all_to_all x1, starting transfers between devices, per_device(): lax.all_to_all(produced.astype(jnp.bfloat16), 'ep', split_axis=0, concat_...  15.6 us
    pmax x1, blocking collectives, per_device(): top_all = lax.pmax(peak_score, 'ctx')  14.3 us
  transfers between devices with their start and end apart: 4, of which 4 were waited for; matrix products, arithmetic and copies ran while one was open for 1% of the time, Pallas kernels for 0%

commit v1 on v0

v1 whole, which is shorter than its diff:
```python
import jax
import jax.numpy as jnp
from jax import lax
from jax.experimental import pallas as pl
from jax.experimental.pallas import tpu as pltpu
from jax.sharding import PartitionSpec as P

D = 7168
LAT = 512
KDIM = 576
TOP = 8
N_CTX = 8
N_Y = 4
N_Z = 16
COLS = 896
NJ = 7
HALF = 512

score_scale = 192.0 ** (-0.5)
epsilon = 1e-06
very_low = -1e30

MESH = pl.DeviceIdType.MESH
F32 = jnp.float32
BF16 = jnp.bfloat16


def dot(a, b):
    return jnp.dot(a, b, preferred_element_type=F32)


def dot_nt(a, b):
    return lax.dot_general(a, b, (((1,), (1,)), ((), ())), preferred_element_type=F32)


def iota(shape, dim):
    return lax.broadcasted_iota(jnp.int32, shape, dim)


def three_parts(x, shape):
    hi = x.astype(BF16).astype(F32)
    mid = (x - hi).astype(BF16).astype(F32)
    low = x - hi - mid
    lane = iota(shape, 1)
    zero = jnp.zeros(shape, F32)
    return jnp.where(lane == 0, hi, jnp.where(lane == 1, mid, jnp.where(lane == 2, low, zero)))


def kernel(
    page_table,
    lengths,
    routes,
    route_weight,
    new_key,
    hidden,
    gain,
    queries,
    cache,
    w_uv,
    w_out,
    w_gate,
    w_up,
    w_down,
    attn_out,
    layer_out,
    q_vm,
    cache_vm,
    wuv_vm,
    wout_vm,
    gate_vm,
    up_vm,
    down_vm,
    nk_scr,
    att_scr,
    tile_scr,
    lhs_scr,
    wide_scr,
    z_scr,
    small_scr,
    hid_scr,
    gain_scr,
    res_scr,
    col_scr,
    sel_scr,
    comb_scr,
    info_send,
    info_recv,
    p2_send,
    p2_recv,
    p3_send,
    p3_recv,
    p4_send,
    p4_recv,
    p5_send,
    p5_recv,
    p6_send,
    p6_recv,
    p6b_send,
    xe,
    p7_send,
    p7_recv,
    p8_send,
    mid_all,
    p9_send,
    p9_recv,
    p10_send,
    p10_recv,
    lsem,
    wo_s,
    wo_r,
    info_s,
    info_r,
    p2_s,
    p2_r,
    p3_s,
    p3_r,
    p4_s,
    p4_r,
    p5_s,
    p5_r,
    p6_s,
    p6_r,
    p6b_s,
    p6b_r,
    p7_s,
    p7_r,
    p8_s,
    p8_r,
    p9_s,
    p9_r,
    p10_s,
    p10_r,
):
    c = lax.axis_index("ctx")
    ep = lax.axis_index("ep")
    y = ep // N_Z
    z = ep % N_Z
    g = ep // 8
    s8 = ep % 8

    def remote(src, dst, ssem, rsem, to_ctx, to_ep):
        return pltpu.make_async_remote_copy(
            src_ref=src,
            dst_ref=dst,
            send_sem=ssem,
            recv_sem=rsem,
            device_id={"ctx": to_ctx, "ep": to_ep},
            device_id_type=MESH,
        )

    def each(count, step):
        def body(i, carry):
            step(i)
            return carry

        lax.fori_loop(0, count, body, 0)

    loads = [
        pltpu.make_async_copy(src, dst, lsem.at[i])
        for i, (src, dst) in enumerate(
            [
                (queries, q_vm),
                (cache, cache_vm),
                (w_uv, wuv_vm),
                (w_out, wout_vm.at[y]),
                (w_gate, gate_vm),
                (w_up, up_vm),
                (w_down, down_vm),
            ]
        )
    ]
    for load in loads:
        load.start()

    barrier = pltpu.get_barrier_semaphore()

    def greet(to_ctx, to_ep):
        pl.semaphore_signal(
            barrier, inc=1, device_id={"ctx": to_ctx, "ep": to_ep}, device_id_type=MESH
        )

    def greet_plane(i):
        k = i + 1
        greet((c + k % N_CTX) % N_CTX, (y + k // N_CTX) % N_Y * N_Z + z)

    each(N_CTX * N_Y - 1, greet_plane)
    each(N_Z - 1, lambda i: greet(c, y * N_Z + (z + i + 1) % N_Z))

    def greet_swap(i):
        @pl.when(jnp.logical_not((c == g) & (i == s8)))
        def _():
            greet(g, c * 8 + i)

    each(8, greet_swap)

    row = iota((32, 128), 0)
    expert = (row // 2) % 4 * 4 + row // 8
    place = row % 2
    before = jnp.zeros((32, 128), jnp.int32)
    pick = jnp.zeros((32, 128), F32)
    weight = jnp.zeros((32, 128), F32)
    for r in range(4):
        named = jnp.zeros((32, 128), jnp.int32)
        w_r = jnp.zeros((32, 128), F32)
        for k in range(TOP):
            hit = expert == routes[r, k]
            named = jnp.where(hit, 1, named)
            w_r = jnp.where(hit, route_weight[r, k], w_r)
        taken = (named == 1) & (before == place)
        pick = jnp.where(taken, float(r), pick)
        weight = jnp.where(taken, w_r, weight)
        before = before + named
    info = jnp.where(iota((32, 128), 1) < 64, pick, weight)
    info_send[...] = info.reshape(4, 8, 128)
    info_recv[z] = info_send[z // 4]

    small_scr[0:4, :] = jnp.zeros((4, 128), F32)
    hid_scr[28:32, :] = jnp.zeros((4, 128), F32)
    gain_scr[28:32, :] = jnp.zeros((4, 128), F32)
    hid32 = hidden[...].astype(F32)
    for j in range(NJ):
        hid_scr[4 * j : 4 * j + 4, :] = hid32[:, 128 * j : 128 * j + 128]
        gain_scr[4 * j : 4 * j + 4, :] = jnp.broadcast_to(
            gain[:, 128 * j : 128 * j + 128], (4, 128)
        )
    nk_scr[...] = jnp.zeros((128, KDIM), BF16)
    nk_scr[0:4, :] = new_key[...]
    for zz in range(N_Z):
        z_scr[32 * zz + 28 : 32 * zz + 32, :] = jnp.zeros((4, 128), F32)

    col = iota((1, 1024), 1)
    slot = col // 64
    owner = jnp.full((1, 1024), -1, jnp.int32)
    for r in range(4):
        for p in range(4):
            position = (p * N_CTX + c) * 64 + col % 64
            good = (slot == page_table[r, 0, p]) & (position < lengths[r])
            owner = jnp.where(good, r, owner)
    i0 = iota((256, 256), 0)
    shuffle = jnp.where((i0 % 4) * 64 + i0 // 4 == iota((256, 256), 1), 1.0, 0.0).astype(BF16)
    loads[0].wait()
    q = dot(shuffle, q_vm[...].reshape(256, KDIM)).astype(BF16)
    loads[1].wait()
    keys = cache_vm[...].reshape(1024, KDIM)
    scores = dot_nt(q, keys) * score_scale
    fresh = dot_nt(q, nk_scr[...]) * score_scale
    mask = owner == iota((256, 1024), 0) % 4
    mask_new = iota((256, 128), 1) + 1024 * c == iota((256, 128), 0) % 4
    peak = jnp.maximum(
        jnp.max(jnp.where(mask, scores, very_low), axis=1, keepdims=True),
        jnp.max(jnp.where(mask_new, fresh, very_low), axis=1, keepdims=True),
    )
    weights = jnp.where(mask, jnp.exp(scores - peak), 0.0).astype(BF16)
    weights_new = jnp.where(mask_new, jnp.exp(fresh - peak), 0.0).astype(BF16)
    total = jnp.sum(weights.astype(F32), axis=1, keepdims=True) + jnp.sum(
        weights_new.astype(F32), axis=1, keepdims=True
    )
    mixture = dot(weights, keys[:, :LAT]) + dot(weights_new, nk_scr[:, :LAT])
    some = total > 0.0
    total = jnp.where(some, total, 1.0)
    logsum = jnp.where(some, peak + jnp.log(total), very_low)
    p2_send[:, :, :LAT] = (mixture / total).astype(BF16).reshape(N_CTX, 32, LAT)
    p2_send[:, :, LAT:] = three_parts(logsum, (256, 128)).astype(BF16).reshape(N_CTX, 32, 128)

    pl.semaphore_wait(
        barrier, N_CTX * N_Y - 1 + N_Z - 1 + 8 - jnp.where(c == g, 1, 0).astype(jnp.int32)
    )

    def p2_copy(i):
        to = (c + i + 1) % N_CTX
        return remote(p2_send.at[to], p2_recv.at[i], p2_s.at[i], p2_r.at[i], to, ep)

    each(N_CTX - 1, lambda i: p2_copy(i).start())

    def info_copy(i):
        to = (z + i + 1) % N_Z
        return remote(
            info_send.at[to // 4], info_recv.at[z], info_s.at[i], info_r.at[i], c, y * N_Z + to
        )

    def info_arrival(i):
        frm = (z + N_Z - i - 1) % N_Z
        return remote(info_send.at[0], info_recv.at[frm], info_s.at[i], info_r.at[i], c, y * N_Z + frm)

    each(N_Z - 1, lambda i: info_copy(i).start())

    def wo_copy(i):
        to = (y + i + 1) % N_Y
        return remote(w_out, wout_vm.at[y], wo_s.at[i], wo_r.at[i], c, to * N_Z + z)

    def wo_arrival(i):
        frm = (y + N_Y - i - 1) % N_Y
        return remote(w_out, wout_vm.at[frm], wo_s.at[i], wo_r.at[i], c, frm * N_Z + z)

    each(N_Y - 1, lambda i: wo_copy(i).start())

    each(N_CTX - 1, lambda i: p2_copy(i).wait_recv())
    parts = [p2_send[c]] + [p2_recv[i] for i in range(N_CTX - 1)]
    logs = [jnp.sum(p[:, LAT:].astype(F32), axis=1, keepdims=True) for p in parts]
    top = logs[0]
    for l in logs[1:]:
        top = jnp.maximum(top, l)
    above = jnp.zeros((32, LAT), F32)
    below = jnp.zeros((32, 1), F32)
    for p, l in zip(parts, logs):
        f = jnp.exp(l - top)
        above = above + f * p[:, :LAT].astype(F32)
        below = below + f
    att_scr[...] = above / below
    for i in range(8):
        for j in range(4):
            tile_scr[16 * i + 4 * j : 16 * i + 4 * j + 4, :] = att_scr[
                4 * i : 4 * i + 4, 128 * j : 128 * j + 128
            ]
    p3_send[...] = tile_scr[...].astype(BF16).reshape(8, 16, 128)

    def p3_copy(i):
        return remote(
            p3_send.at[i], p3_recv.at[s8], p3_s.at[i], p3_r.at[s8], g, c * 8 + i
        )

    def p3_arrival(i):
        return remote(p3_send.at[i], p3_recv.at[i], p3_s.at[i], p3_r.at[i], g, c * 8 + i)

    def p3_each(step):
        def one(i):
            @pl.when(jnp.logical_not((c == g) & (i == s8)))
            def _():
                step(i)

        each(8, one)

    p3_each(lambda i: p3_copy(i).start())

    @pl.when(c == g)
    def _():
        p3_recv[s8] = p3_send[s8]

    loads[2].wait()
    p3_each(lambda i: p3_arrival(i).wait_recv())
    tile_scr[...] = p3_recv[...].astype(F32).reshape(128, 128)
    for i in range(8):
        for j in range(4):
            lhs_scr[4 * i : 4 * i + 4, 128 * j : 128 * j + 128] = tile_scr[
                16 * i + 4 * j : 16 * i + 4 * j + 4, :
            ]
    values = dot(lhs_scr[...].astype(BF16), wuv_vm[0]).astype(BF16)
    p4_send[...] = values

    home = c // 2
    mine = home == y
    slot4 = y * 2 + c % 2

    def p4_copy(i):
        return remote(p4_send, p4_recv.at[slot4], p4_s.at[i], p4_r.at[slot4], i, home * N_Z + z)

    def p4_arrival(i):
        return remote(
            p4_send, p4_recv.at[i], p4_s.at[i], p4_r.at[i], y * 2 + i % 2, i // 2 * N_Z + z
        )

    def p4_sends(step):
        def one(i):
            @pl.when(jnp.logical_not(mine & (i == c)))
            def _():
                step(i)

        each(8, one)

    def p4_arrives(step):
        def one(i):
            @pl.when(jnp.logical_not(mine & (i == slot4)))
            def _():
                step(i)

        each(8, one)

    p4_sends(lambda i: p4_copy(i).start())

    @pl.when(mine)
    def _():
        p4_recv[slot4] = p4_send[...]

    each(N_Z - 1, lambda i: info_arrival(i).wait_recv())
    for k in range(8):
        col_scr[16 * k : 16 * k + 16, :] = info_recv[:, k, :]
    pick_col = col_scr[:, 0:1].astype(jnp.int32)
    weight_col = col_scr[:, 64:65]
    source = iota((128, 1), 0) % 16
    target = source * 32 + pick_col
    lane = iota((128, 512), 1)
    for j in range(8):
        sel_scr[128 * j : 128 * j + 128, :] = jnp.where(lane == target + 4 * j, 1.0, 0.0).astype(BF16)
    spread = jnp.where(iota((128, 128), 1) == source * 4 + pick_col, weight_col, 0.0)
    comb = jnp.transpose(spread)[0:64, :]
    comb_hi = comb.astype(BF16)
    comb_scr[0] = comb_hi
    comb_scr[1] = (comb - comb_hi.astype(F32)).astype(BF16)

    loads[3].wait()
    each(N_Y - 1, lambda i: wo_arrival(i).wait_recv())
    p4_arrives(lambda i: p4_arrival(i).wait_recv())
    lhs = jnp.concatenate(
        [p4_recv[2 * k : 2 * k + 2].reshape(64, 128) for k in range(N_Y)], axis=1
    )

    def to_tiles(values32, send):
        wide_scr[...] = values32
        for zz in range(N_Z):
            for j in range(NJ):
                z_scr[32 * zz + 4 * j : 32 * zz + 4 * j + 4, :] = wide_scr[
                    4 * zz : 4 * zz + 4, 128 * j : 128 * j + 128
                ]
        send[...] = z_scr[...].astype(BF16).reshape(N_Z, 32, 128)

    def z_scatter(send, recv, ssem, rsem):
        def copy(i):
            to = (z + i + 1) % N_Z
            return remote(send.at[to], recv.at[i], ssem.at[i], rsem.at[i], c, y * N_Z + to)

        each(N_Z - 1, lambda i: copy(i).start())
        each(N_Z - 1, lambda i: copy(i).wait_recv())
        total = z_scr[pl.ds(pl.multiple_of(z * 32, 32), 32), :]
        for i in range(N_Z - 1):
            total = total + recv[i].astype(F32)
        return total, copy

    to_tiles(dot(lhs, wout_vm[...].reshape(512, COLS)), p5_send)
    attention, p5_copy = z_scatter(p5_send, p5_recv, p5_s, p5_r)
    residual = hid_scr[...] + attention
    res_scr[...] = residual
    small_scr[...] = residual * residual
    squares = small_scr[0:4, :]
    for j in range(1, NJ):
        squares = squares + small_scr[4 * j : 4 * j + 4, :]
    squares = jnp.sum(squares, axis=1, keepdims=True)
    small_scr[...] = residual * gain_scr[...]
    small_scr[28:32, :] = three_parts(squares, (4, 128))
    scaled = small_scr[...].astype(BF16)
    p6_send[...] = scaled
    p6_recv[z] = scaled

    def p6_copy(i):
        to = (z + i + 1) % N_Z
        return remote(p6_send, p6_recv.at[z], p6_s.at[i], p6_r.at[i], c, y * N_Z + to)

    def p6_arrival(i):
        frm = (z + N_Z - i - 1) % N_Z
        return remote(p6_send, p6_recv.at[frm], p6_s.at[i], p6_r.at[i], c, y * N_Z + frm)

    each(N_Z - 1, lambda i: p6_copy(i).start())
    small_scr[...] = attention
    for j in range(NJ):
        attn_out[:, 128 * j : 128 * j + 128] = small_scr[4 * j : 4 * j + 4, :].astype(BF16)
    each(N_Z - 1, lambda i: p6_arrival(i).wait_recv())

    picked = dot(sel_scr[...], p6_recv[...].reshape(512, 128)).astype(BF16)
    for j in range(8):
        p6b_send[:, :, 128 * j : 128 * j + 128] = picked[128 * j : 128 * j + 128, :].reshape(
            N_Y, 32, 128
        )

    def y_copy(send, recv, ssem, rsem):
        def copy(i):
            to = (y + i + 1) % N_Y
            return remote(send.at[to], recv.at[y], ssem.at[i], rsem.at[i], c, to * N_Z + z)

        def arrival(i):
            frm = (y + N_Y - i - 1) % N_Y
            return remote(send.at[y], recv.at[frm], ssem.at[i], rsem.at[i], c, frm * N_Z + z)

        each(N_Y - 1, lambda i: copy(i).start())
        recv[y] = send[y]
        each(N_Y - 1, lambda i: arrival(i).wait_recv())
        return copy

    p6b_copy = y_copy(p6b_send, xe, p6b_s, p6b_r)

    rows = xe[...].reshape(128, 1024)
    loads[4].wait()
    loads[5].wait()
    p7_send[:, :, :HALF] = dot(rows[:, :COLS], gate_vm[...]).astype(BF16).reshape(N_CTX, 16, HALF)
    p7_send[:, :, HALF : 2 * HALF] = (
        dot(rows[:, :COLS], up_vm[...]).astype(BF16).reshape(N_CTX, 16, HALF)
    )
    p7_send[:, :, 2 * HALF :] = rows[:, COLS:].reshape(N_CTX, 16, 128)

    def p7_copy(i):
        to = (c + i + 1) % N_CTX
        return remote(p7_send.at[to], p7_recv.at[i], p7_s.at[i], p7_r.at[i], to, ep)

    each(N_CTX - 1, lambda i: p7_copy(i).start())
    each(N_CTX - 1, lambda i: p7_copy(i).wait_recv())
    sums = p7_send[c].astype(F32)
    for i in range(N_CTX - 1):
        sums = sums + p7_recv[i].astype(F32)
    mean = jnp.sum(sums[:, 2 * HALF :], axis=1, keepdims=True) / D
    scale = lax.rsqrt(mean + epsilon)
    gate = sums[:, :HALF] * scale
    up = sums[:, HALF : 2 * HALF] * scale
    middle = (gate / (1.0 + jnp.exp(-gate)) * up).astype(BF16)
    p8_send[...] = middle
    mid_all[c] = middle

    def p8_copy(i):
        to = (c + i + 1) % N_CTX
        return remote(p8_send, mid_all.at[c], p8_s.at[i], p8_r.at[i], to, ep)

    def p8_arrival(i):
        frm = (c + N_CTX - i - 1) % N_CTX
        return remote(p8_send, mid_all.at[frm], p8_s.at[i], p8_r.at[i], frm, ep)

    each(N_CTX - 1, lambda i: p8_copy(i).start())
    loads[6].wait()
    each(N_CTX - 1, lambda i: p8_arrival(i).wait_recv())

    produced = dot(mid_all[...].reshape(128, HALF), down_vm[...])
    p9_send[...] = produced.astype(BF16).reshape(N_Y, 32, COLS)
    p9_copy = y_copy(p9_send, p9_recv, p9_s, p9_r)
    back = p9_recv[...].reshape(128, COLS)
    to_tiles(dot(comb_scr[0], back) + dot(comb_scr[1], back), p10_send)
    routed, p10_copy = z_scatter(p10_send, p10_recv, p10_s, p10_r)
    small_scr[...] = res_scr[...] + routed
    for j in range(NJ):
        layer_out[:, 128 * j : 128 * j + 128] = small_scr[4 * j : 4 * j + 4, :].astype(BF16)

    each(N_CTX - 1, lambda i: p2_copy(i).wait_send())
    each(N_Z - 1, lambda i: info_copy(i).wait_send())
    each(N_Y - 1, lambda i: wo_copy(i).wait_send())
    p3_each(lambda i: p3_copy(i).wait_send())
    p4_sends(lambda i: p4_copy(i).wait_send())
    each(N_Z - 1, lambda i: p5_copy(i).wait_send())
    each(N_Z - 1, lambda i: p6_copy(i).wait_send())
    each(N_Y - 1, lambda i: p6b_copy(i).wait_send())
    each(N_CTX - 1, lambda i: p7_copy(i).wait_send())
    each(N_CTX - 1, lambda i: p8_copy(i).wait_send())
    each(N_Y - 1, lambda i: p9_copy(i).wait_send())
    each(N_Z - 1, lambda i: p10_copy(i).wait_send())


def per_device(
    queries,
    new_key,
    latent_cache,
    page_table,
    lengths,
    hidden_in,
    w_uv,
    w_out,
    norm_gain,
    routes,
    route_weight,
    w_gate,
    w_up,
    w_down,
):
    smem = pl.BlockSpec(memory_space=pltpu.SMEM)
    vmem = pl.BlockSpec(memory_space=pltpu.VMEM)
    anywhere = pl.BlockSpec(memory_space=pl.ANY)
    dma = pltpu.SemaphoreType.DMA
    scratch = [
        pltpu.VMEM((4, 64, KDIM), BF16),
        pltpu.VMEM((1, 16, 64, KDIM), BF16),
        pltpu.VMEM((1, LAT, 128), BF16),
        pltpu.VMEM((N_Y, 128, COLS), BF16),
        pltpu.VMEM((COLS, HALF), BF16),
        pltpu.VMEM((COLS, HALF), BF16),
        pltpu.VMEM((HALF, COLS), BF16),
        pltpu.VMEM((128, KDIM), BF16),
        pltpu.VMEM((32, LAT), F32),
        pltpu.VMEM((128, 128), F32),
        pltpu.VMEM((32, LAT), F32),
        pltpu.VMEM((64, COLS), F32),
        pltpu.VMEM((512, 128), F32),
        pltpu.VMEM((32, 128), F32),
        pltpu.VMEM((32, 128), F32),
        pltpu.VMEM((32, 128), F32),
        pltpu.VMEM((32, 128), F32),
        pltpu.VMEM((128, 128), F32),
        pltpu.VMEM((1024, 512), BF16),
        pltpu.VMEM((2, 64, 128), BF16),
        pltpu.VMEM((4, 8, 128), F32),
        pltpu.VMEM((N_Z, 8, 128), F32),
        pltpu.VMEM((N_CTX, 32, 640), BF16),
        pltpu.VMEM((N_CTX - 1, 32, 640), BF16),
        pltpu.VMEM((8, 16, 128), BF16),
        pltpu.VMEM((8, 16, 128), BF16),
        pltpu.VMEM((32, 128), BF16),
        pltpu.VMEM((8, 32, 128), BF16),
        pltpu.VMEM((N_Z, 32, 128), BF16),
        pltpu.VMEM((N_Z - 1, 32, 128), BF16),
        pltpu.VMEM((32, 128), BF16),
        pltpu.VMEM((N_Z, 32, 128), BF16),
        pltpu.VMEM((N_Y, 32, 1024), BF16),
        pltpu.VMEM((N_Y, 32, 1024), BF16),
        pltpu.VMEM((N_CTX, 16, 1152), BF16),
        pltpu.VMEM((N_CTX - 1, 16, 1152), BF16),
        pltpu.VMEM((16, HALF), BF16),
        pltpu.VMEM((N_CTX, 16, HALF), BF16),
        pltpu.VMEM((N_Y, 32, COLS), BF16),
        pltpu.VMEM((N_Y, 32, COLS), BF16),
        pltpu.VMEM((N_Z, 32, 128), BF16),
        pltpu.VMEM((N_Z - 1, 32, 128), BF16),
        dma((7,)),
    ]
    for count in (3, 15, 7, 8, 8, 15, 15, 3, 7, 7, 3, 15):
        scratch += [dma((count,)), dma((count,))]
    out = jax.ShapeDtypeStruct((4, COLS), BF16)
    return pl.pallas_call(
        kernel,
        out_shape=(out, out),
        in_specs=[smem] * 4 + [vmem] * 3 + [anywhere] * 7,
        out_specs=(vmem, vmem),
        scratch_shapes=scratch,
        compiler_params=pltpu.CompilerParams(
            collective_id=0, has_side_effects=True, vmem_limit_bytes=40 * 1024 * 1024
        ),
    )(
        page_table,
        lengths,
        routes,
        route_weight,
        new_key,
        hidden_in,
        norm_gain.reshape(1, COLS),
        queries,
        latent_cache,
        w_uv,
        w_out,
        w_gate,
        w_up,
        w_down,
    )


def solution(mesh):
    placed = (
        P("ep", None, None),
        P("ep", None),
        P("ctx", "ep", None, None),
        P("ep", "ctx", None),
        P("ep"),
        P("ep", "ctx"),
        P("ep", None, None),
        P("ep", "ctx"),
        P("ctx"),
        P("ep", None),
        P("ep", None),
        P("ctx", "ep"),
        P("ctx", "ep"),
        P("ep", "ctx"),
    )
    return jax.shard_map(
        per_device,
        mesh=mesh,
        in_specs=placed,
        out_specs=(P("ep", "ctx"), P("ep", "ctx")),
        check_vma=False,
    )
```

time: 565 us -> 108 us (0.19)
  the two profiles are of different devices: /device:TPU:6 before, /device:TPU:1 now
where the time goes in v1:
time: 108 us; the launch traced here: 107 us
  Pallas kernels  92.7 us (86%)
  local copies, waits for them, and re-layouts  13.6 us (13%)
    pallas_call x1, Pallas kernels, per_device(): pl.pallas_call(kernel, out_shape=(out, out), in_specs=[smem] * 4 + [vmem]...  92.7 us
    unnamed x28, local copies, waits for them, and re-layouts  12.9 us

profile of v1, /device:TPU:1, one launch (start us, length us, event | category | flops | bytes accessed | tf_op | source)
XLA Modules:
  0.0 107.0 jit_solution(17176555757496925627)
XLA Ops:
  0.6 0.7 reshape.7.gain
  1.3 0.0 copy-start
  1.3 1.3 %copy-done = bf16[1,16,64,576]{3,2,1,0:T(8,128)(2,1)S(1)} copy-done((bf16[1,16,64,576]{3,2,1,0:T(8,128)(2,1)S(1)}, bf16[1,16,64,576]{3,2,1,0:T(8,128)(2,1)}, u32[]{:S(2)}) %copy-start) | copy-done | bytes 1179672
  2.6 0.0 copy-start.1
  2.6 1.2 %copy-done.1 = bf16[896,512]{1,0:T(8,128)(2,1)S(1)} copy-done((bf16[896,512]{1,0:T(8,128)(2,1)S(1)}, bf16[896,512]{1,0:T(8,128)(2,1)}, u32[]{:S(2)}) %copy-start.1) | copy-done | bytes 917528
  3.8 0.0 copy-start.2
  3.8 1.2 %copy-done.2 = bf16[896,512]{1,0:T(8,128)(2,1)S(1)} copy-done((bf16[896,512]{1,0:T(8,128)(2,1)S(1)}, bf16[896,512]{1,0:T(8,128)(2,1)}, u32[]{:S(2)}) %copy-start.2) | copy-done | bytes 917528
  5.0 0.0 copy-start.3
  5.0 1.2 %copy-done.3 = bf16[512,896]{1,0:T(8,128)(2,1)S(1)} copy-done((bf16[512,896]{1,0:T(8,128)(2,1)S(1)}, bf16[512,896]{1,0:T(8,128)(2,1)}, u32[]{:S(2)}) %copy-start.3) | copy-done | bytes 917528
  6.2 0.0 copy-start.4
  6.2 1.0 copy-done.4
  7.1 0.0 copy-start.5
  7.2 0.9 copy-done.5
  8.1 0.0 copy-start.6
  8.1 0.9 copy-done.6
  9.0 0.0 copy-start.7
  9.0 0.7 copy-done.7
  9.7 0.0 copy-start.8
  9.7 0.7 copy-done.8
  10.4 0.0 copy-start.9
  10.4 0.7 copy-done.9
  11.1 0.0 copy-start.10
  11.1 0.7 copy-done.10
  11.7 0.0 copy-start.11
  11.7 0.7 copy-done.11
  12.4 0.0 copy-start.12
  12.4 0.7 copy-done.12
  13.1 92.7 %shard_map.149 = (bf16[4,896]{1,0:T(4,128)(2,1)S(1)}, bf16[4,896]{1,0:T(4,128)(2,1)S(1)}) custom-call(s32[4,1,4]{2,1,0:T(1,128)S(1)} %copy-done.9, s32[4]{0:T(128)S(1)} %copy-done.12, s32[4,8]{1,0:T(4,128)S(1)} %copy-done.10, f32[4,8]{1,0:T(4,128)S(1)} %copy-done.11, bf16[4,576]{1,0:T(4,128)(2,1)S(1)} %copy-done.8, bf16[4,896]{1,0:T(4,128)(2,1)S(1)} %copy-done.7, ...), custom_call_target="tpu_custom_call" | custom-call | tf_op jit(solution)/shard_map/pallas_call | solution.py:609
  105.8 0.6 copy.18
  106.4 0.6 copy.19
Async XLA Ops:
  1.3 1.3 %copy-start = (bf16[1,16,64,576]{3,2,1,0:T(8,128)(2,1)S(1)}, bf16[1,16,64,576]{3,2,1,0:T(8,128)(2,1)}, u32[]{:S(2)}) copy-start(bf16[1,16,64,576]{3,2,1,0:T(8,128)(2,1)} %cache.1) | copy-start | bytes 3538948
  2.6 1.2 %copy-start.1 = (bf16[896,512]{1,0:T(8,128)(2,1)S(1)}, bf16[896,512]{1,0:T(8,128)(2,1)}, u32[]{:S(2)}) copy-start(bf16[896,512]{1,0:T(8,128)(2,1)} %w_gate.1) | copy-start | bytes 2752516
  3.8 1.2 %copy-start.2 = (bf16[896,512]{1,0:T(8,128)(2,1)S(1)}, bf16[896,512]{1,0:T(8,128)(2,1)}, u32[]{:S(2)}) copy-start(bf16[896,512]{1,0:T(8,128)(2,1)} %w_up.1) | copy-start | bytes 2752516
  5.0 1.2 %copy-start.3 = (bf16[512,896]{1,0:T(8,128)(2,1)S(1)}, bf16[512,896]{1,0:T(8,128)(2,1)}, u32[]{:S(2)}) copy-start(bf16[512,896]{1,0:T(8,128)(2,1)} %w_down.1) | copy-start | bytes 2752516
  6.2 1.0 copy-start.4
  7.1 0.9 copy-start.5
  8.1 0.9 copy-start.6
  9.0 0.7 copy-start.7
  9.7 0.7 copy-start.8
  10.4 0.7 copy-start.9
  11.1 0.7 copy-start.10
  11.7 0.7 copy-start.11
  12.4 0.7 copy-start.12

commit v2 on v1

--- a/solution.py
+++ b/solution.py
@@ -47,13 +47,13 @@
 
 
 def kernel(
-    page_table,
-    lengths,
-    routes,
-    route_weight,
-    new_key,
-    hidden,
-    gain,
+    page_table_in,
+    lengths_in,
+    routes_in,
+    route_weight_in,
+    new_key_in,
+    hidden_in,
+    gain_in,
     queries,
     cache,
     w_uv,
@@ -63,6 +63,13 @@
     w_down,
     attn_out,
     layer_out,
+    page_table,
+    lengths,
+    routes,
+    route_weight,
+    new_key,
+    hidden,
+    gain,
     q_vm,
     cache_vm,
     wuv_vm,
@@ -166,11 +173,29 @@
                 (w_gate, gate_vm),
                 (w_up, up_vm),
                 (w_down, down_vm),
+                (page_table_in, page_table),
+                (lengths_in, lengths),
+                (routes_in, routes),
+                (route_weight_in, route_weight),
+                (new_key_in, new_key),
+                (hidden_in, hidden),
+                (gain_in, gain),
             ]
         )
     ]
-    for load in loads:
+    for load in loads[:2] + loads[7:] + loads[2:7]:
         load.start()
+    pending = []
+
+    def finish():
+        for wait in pending:
+            wait()
+
+    def landed(buffer, sem):
+        pltpu.make_async_copy(buffer, buffer, sem).wait()
+
+    def z_step(i):
+        return 8 + (i + 1) // 2 * (1 - 2 * (i % 2))
 
     barrier = pltpu.get_barrier_semaphore()
 
@@ -183,18 +208,18 @@
         k = i + 1
         greet((c + k % N_CTX) % N_CTX, (y + k // N_CTX) % N_Y * N_Z + z)
 
+    g_to = (g + 4) % 8
+    c_from = (c + 4) % 8
+    each(N_Z - 1, lambda i: greet(c, y * N_Z + (z + z_step(i)) % N_Z))
+    each(8, lambda i: greet(g_to, c * 8 + i))
+    each(8, lambda i: greet(g, c_from * 8 + i))
     each(N_CTX * N_Y - 1, greet_plane)
-    each(N_Z - 1, lambda i: greet(c, y * N_Z + (z + i + 1) % N_Z))
-
-    def greet_swap(i):
-        @pl.when(jnp.logical_not((c == g) & (i == s8)))
-        def _():
-            greet(g, c * 8 + i)
-
-    each(8, greet_swap)
+
+    for load in loads[7:]:
+        load.wait()
 
     row = iota((32, 128), 0)
-    expert = (row // 2) % 4 * 4 + row // 8
+    expert = ((row // 2) % 4 + y) % 4 * 4 + row // 8
     place = row % 2
     before = jnp.zeros((32, 128), jnp.int32)
     pick = jnp.zeros((32, 128), F32)
@@ -212,7 +237,7 @@
         before = before + named
     info = jnp.where(iota((32, 128), 1) < 64, pick, weight)
     info_send[...] = info.reshape(4, 8, 128)
-    info_recv[z] = info_send[z // 4]
+    info_recv[0] = info_send[z // 4]
 
     small_scr[0:4, :] = jnp.zeros((4, 128), F32)
     hid_scr[28:32, :] = jnp.zeros((4, 128), F32)
@@ -221,7 +246,7 @@
     for j in range(NJ):
         hid_scr[4 * j : 4 * j + 4, :] = hid32[:, 128 * j : 128 * j + 128]
         gain_scr[4 * j : 4 * j + 4, :] = jnp.broadcast_to(
-            gain[:, 128 * j : 128 * j + 128], (4, 128)
+            gain[128 * j : 128 * j + 128].reshape(1, 128), (4, 128)
         )
     nk_scr[...] = jnp.zeros((128, KDIM), BF16)
     nk_scr[0:4, :] = new_key[...]
@@ -262,39 +287,51 @@
     p2_send[:, :, :LAT] = (mixture / total).astype(BF16).reshape(N_CTX, 32, LAT)
     p2_send[:, :, LAT:] = three_parts(logsum, (256, 128)).astype(BF16).reshape(N_CTX, 32, 128)
 
-    pl.semaphore_wait(
-        barrier, N_CTX * N_Y - 1 + N_Z - 1 + 8 - jnp.where(c == g, 1, 0).astype(jnp.int32)
-    )
-
-    def p2_copy(i):
-        to = (c + i + 1) % N_CTX
-        return remote(p2_send.at[to], p2_recv.at[i], p2_s.at[i], p2_r.at[i], to, ep)
-
-    each(N_CTX - 1, lambda i: p2_copy(i).start())
+    pl.semaphore_wait(barrier, N_CTX * N_Y - 1 + N_Z - 1 + 16)
+
+    def ctx_step(k):
+        return (c // 2 + k // 2) % 4 * 2 + (c + k) % 2
+
+    def ctx_back(k):
+        return (c // 2 + 4 - k // 2) % 4 * 2 + (c + k) % 2
+
+    ctx_order = (4, 5, 2, 3, 6, 7, 1)
+    y_order = (2, 1, 3)
+
+    def ctx_scatter(send, recv, ssem, rsem):
+        for k in ctx_order:
+            to = ctx_step(k)
+            remote(send.at[to], recv.at[k - 1], ssem, rsem, to, ep).start()
+        pending.append(lambda: landed(recv, ssem))
+
+    ctx_scatter(p2_send, p2_recv, p2_s, p2_r)
 
     def info_copy(i):
-        to = (z + i + 1) % N_Z
-        return remote(
-            info_send.at[to // 4], info_recv.at[z], info_s.at[i], info_r.at[i], c, y * N_Z + to
-        )
-
-    def info_arrival(i):
-        frm = (z + N_Z - i - 1) % N_Z
-        return remote(info_send.at[0], info_recv.at[frm], info_s.at[i], info_r.at[i], c, y * N_Z + frm)
-
-    each(N_Z - 1, lambda i: info_copy(i).start())
-
-    def wo_copy(i):
-        to = (y + i + 1) % N_Y
-        return remote(w_out, wout_vm.at[y], wo_s.at[i], wo_r.at[i], c, to * N_Z + z)
-
-    def wo_arrival(i):
-        frm = (y + N_Y - i - 1) % N_Y
-        return remote(w_out, wout_vm.at[frm], wo_s.at[i], wo_r.at[i], c, frm * N_Z + z)
-
-    each(N_Y - 1, lambda i: wo_copy(i).start())
-
-    each(N_CTX - 1, lambda i: p2_copy(i).wait_recv())
+        step = z_step(i)
+        to = (z + step) % N_Z
+        remote(
+            info_send.at[to // 4], info_recv.at[step], info_s, info_r, c, y * N_Z + to
+        ).start()
+
+    each(N_Z - 1, info_copy)
+    pending.append(lambda: landed(info_recv.at[1:N_Z], info_s))
+
+    for k in y_order:
+        remote(
+            w_out, wout_vm.at[y], wo_s.at[k - 1], wo_r.at[k - 1], c, (y + k) % N_Y * N_Z + z
+        ).start()
+    for k in y_order:
+        pending.append(
+            remote(
+                w_out, wout_vm.at[y], wo_s.at[k - 1], wo_r.at[k - 1], c, (y + k) % N_Y * N_Z + z
+            ).wait_send
+        )
+
+    def wo_arrival(k):
+        frm = (y + N_Y - k) % N_Y
+        return remote(w_out, wout_vm.at[frm], wo_s.at[k - 1], wo_r.at[k - 1], c, frm * N_Z + z)
+
+    landed(p2_recv, p2_r)
     parts = [p2_send[c]] + [p2_recv[i] for i in range(N_CTX - 1)]
     logs = [jnp.sum(p[:, LAT:].astype(F32), axis=1, keepdims=True) for p in parts]
     top = logs[0]
@@ -314,30 +351,12 @@
             ]
     p3_send[...] = tile_scr[...].astype(BF16).reshape(8, 16, 128)
 
-    def p3_copy(i):
-        return remote(
-            p3_send.at[i], p3_recv.at[s8], p3_s.at[i], p3_r.at[s8], g, c * 8 + i
-        )
-
-    def p3_arrival(i):
-        return remote(p3_send.at[i], p3_recv.at[i], p3_s.at[i], p3_r.at[i], g, c * 8 + i)
-
-    def p3_each(step):
-        def one(i):
-            @pl.when(jnp.logical_not((c == g) & (i == s8)))
-            def _():
-                step(i)
-
-        each(8, one)
-
-    p3_each(lambda i: p3_copy(i).start())
-
-    @pl.when(c == g)
-    def _():
-        p3_recv[s8] = p3_send[s8]
-
+    each(
+        8, lambda i: remote(p3_send.at[i], p3_recv.at[s8], p3_s, p3_r, g_to, c * 8 + i).start()
+    )
+    pending.append(lambda: landed(p3_recv, p3_s))
     loads[2].wait()
-    p3_each(lambda i: p3_arrival(i).wait_recv())
+    landed(p3_recv, p3_r)
     tile_scr[...] = p3_recv[...].astype(F32).reshape(128, 128)
     for i in range(8):
         for j in range(4):
@@ -347,7 +366,7 @@
     values = dot(lhs_scr[...].astype(BF16), wuv_vm[0]).astype(BF16)
     p4_send[...] = values
 
-    home = c // 2
+    home = (c // 2 + 2) % N_Y
     mine = home == y
     slot4 = y * 2 + c % 2
 
@@ -356,7 +375,12 @@
 
     def p4_arrival(i):
         return remote(
-            p4_send, p4_recv.at[i], p4_s.at[i], p4_r.at[i], y * 2 + i % 2, i // 2 * N_Z + z
+            p4_send,
+            p4_recv.at[i],
+            p4_s.at[i],
+            p4_r.at[i],
+            (y + 2) % N_Y * 2 + i % 2,
+            i // 2 * N_Z + z,
         )
 
     def p4_sends(step):
@@ -376,12 +400,13 @@
         each(8, one)
 
     p4_sends(lambda i: p4_copy(i).start())
+    pending.append(lambda: p4_sends(lambda i: p4_copy(i).wait_send()))
 
     @pl.when(mine)
     def _():
         p4_recv[slot4] = p4_send[...]
 
-    each(N_Z - 1, lambda i: info_arrival(i).wait_recv())
+    landed(info_recv.at[1:N_Z], info_r)
     for k in range(8):
         col_scr[16 * k : 16 * k + 16, :] = info_recv[:, k, :]
     pick_col = col_scr[:, 0:1].astype(jnp.int32)
@@ -398,7 +423,8 @@
     comb_scr[1] = (comb - comb_hi.astype(F32)).astype(BF16)
 
     loads[3].wait()
-    each(N_Y - 1, lambda i: wo_arrival(i).wait_recv())
+    for k in y_order:
+        wo_arrival(k).wait_recv()
     p4_arrives(lambda i: p4_arrival(i).wait_recv())
     lhs = jnp.concatenate(
         [p4_recv[2 * k : 2 * k + 2].reshape(64, 128) for k in range(N_Y)], axis=1
@@ -413,20 +439,28 @@
                 ]
         send[...] = z_scr[...].astype(BF16).reshape(N_Z, 32, 128)
 
-    def z_scatter(send, recv, ssem, rsem):
+    def z_scatter(send, own, index, recv, ssem, rsem):
         def copy(i):
-            to = (z + i + 1) % N_Z
-            return remote(send.at[to], recv.at[i], ssem.at[i], rsem.at[i], c, y * N_Z + to)
-
-        each(N_Z - 1, lambda i: copy(i).start())
-        each(N_Z - 1, lambda i: copy(i).wait_recv())
-        total = z_scr[pl.ds(pl.multiple_of(z * 32, 32), 32), :]
+            step = z_step(i)
+            remote(
+                send.at[index(step)],
+                recv.at[step - 1],
+                ssem,
+                rsem,
+                c,
+                y * N_Z + (z + step) % N_Z,
+            ).start()
+
+        each(N_Z - 1, copy)
+        pending.append(lambda: landed(recv, ssem))
+        total = z_scr[pl.ds(pl.multiple_of(own * 32, 32), 32), :]
+        landed(recv, rsem)
         for i in range(N_Z - 1):
             total = total + recv[i].astype(F32)
-        return total, copy
+        return total
 
     to_tiles(dot(lhs, wout_vm[...].reshape(512, COLS)), p5_send)
-    attention, p5_copy = z_scatter(p5_send, p5_recv, p5_s, p5_r)
+    attention = z_scatter(p5_send, z, lambda step: (z + step) % N_Z, p5_recv, p5_s, p5_r)
     residual = hid_scr[...] + attention
     res_scr[...] = residual
     small_scr[...] = residual * residual
@@ -438,21 +472,20 @@
     small_scr[28:32, :] = three_parts(squares, (4, 128))
     scaled = small_scr[...].astype(BF16)
     p6_send[...] = scaled
-    p6_recv[z] = scaled
+    p6_recv[0] = scaled
 
     def p6_copy(i):
-        to = (z + i + 1) % N_Z
-        return remote(p6_send, p6_recv.at[z], p6_s.at[i], p6_r.at[i], c, y * N_Z + to)
-
-    def p6_arrival(i):
-        frm = (z + N_Z - i - 1) % N_Z
-        return remote(p6_send, p6_recv.at[frm], p6_s.at[i], p6_r.at[i], c, y * N_Z + frm)
-
-    each(N_Z - 1, lambda i: p6_copy(i).start())
+        step = z_step(i)
+        remote(
+            p6_send, p6_recv.at[step], p6_s, p6_r, c, y * N_Z + (z + step) % N_Z
+        ).start()
+
+    each(N_Z - 1, p6_copy)
+    pending.append(lambda: landed(p6_recv.at[1:N_Z], p6_s))
     small_scr[...] = attention
     for j in range(NJ):
         attn_out[:, 128 * j : 128 * j + 128] = small_scr[4 * j : 4 * j + 4, :].astype(BF16)
-    each(N_Z - 1, lambda i: p6_arrival(i).wait_recv())
+    landed(p6_recv.at[1:N_Z], p6_r)
 
     picked = dot(sel_scr[...], p6_recv[...].reshape(512, 128)).astype(BF16)
     for j in range(8):
@@ -460,21 +493,16 @@
             N_Y, 32, 128
         )
 
-    def y_copy(send, recv, ssem, rsem):
-        def copy(i):
-            to = (y + i + 1) % N_Y
-            return remote(send.at[to], recv.at[y], ssem.at[i], rsem.at[i], c, to * N_Z + z)
-
-        def arrival(i):
-            frm = (y + N_Y - i - 1) % N_Y
-            return remote(send.at[y], recv.at[frm], ssem.at[i], rsem.at[i], c, frm * N_Z + z)
-
-        each(N_Y - 1, lambda i: copy(i).start())
-        recv[y] = send[y]
-        each(N_Y - 1, lambda i: arrival(i).wait_recv())
-        return copy
-
-    p6b_copy = y_copy(p6b_send, xe, p6b_s, p6b_r)
+    def y_copy(send, recv, ssem, rsem, sign):
+        for k in y_order:
+            remote(
+                send.at[k], recv.at[k], ssem, rsem, c, (y + N_Y + sign * k) % N_Y * N_Z + z
+            ).start()
+        pending.append(lambda: landed(recv.at[1:N_Y], ssem))
+        recv[0] = send[0]
+        landed(recv.at[1:N_Y], rsem)
+
+    y_copy(p6b_send, xe, p6b_s, p6b_r, 1)
 
     rows = xe[...].reshape(128, 1024)
     loads[4].wait()
@@ -485,12 +513,8 @@
     )
     p7_send[:, :, 2 * HALF :] = rows[:, COLS:].reshape(N_CTX, 16, 128)
 
-    def p7_copy(i):
-        to = (c + i + 1) % N_CTX
-        return remote(p7_send.at[to], p7_recv.at[i], p7_s.at[i], p7_r.at[i], to, ep)
-
-    each(N_CTX - 1, lambda i: p7_copy(i).start())
-    each(N_CTX - 1, lambda i: p7_copy(i).wait_recv())
+    ctx_scatter(p7_send, p7_recv, p7_s, p7_r)
+    landed(p7_recv, p7_r)
     sums = p7_send[c].astype(F32)
     for i in range(N_CTX - 1):
         sums = sums + p7_recv[i].astype(F32)
@@ -502,40 +526,32 @@
     p8_send[...] = middle
     mid_all[c] = middle
 
-    def p8_copy(i):
-        to = (c + i + 1) % N_CTX
-        return remote(p8_send, mid_all.at[c], p8_s.at[i], p8_r.at[i], to, ep)
-
-    def p8_arrival(i):
-        frm = (c + N_CTX - i - 1) % N_CTX
-        return remote(p8_send, mid_all.at[frm], p8_s.at[i], p8_r.at[i], frm, ep)
-
-    each(N_CTX - 1, lambda i: p8_copy(i).start())
+    for k in ctx_order:
+        remote(
+            p8_send, mid_all.at[c], p8_s.at[k - 1], p8_r.at[k - 1], ctx_step(k), ep
+        ).start()
+    for k in ctx_order:
+        pending.append(
+            remote(
+                p8_send, mid_all.at[c], p8_s.at[k - 1], p8_r.at[k - 1], ctx_step(k), ep
+            ).wait_send
+        )
     loads[6].wait()
-    each(N_CTX - 1, lambda i: p8_arrival(i).wait_recv())
+    for k in ctx_order:
+        frm = ctx_back(k)
+        remote(p8_send, mid_all.at[frm], p8_s.at[k - 1], p8_r.at[k - 1], frm, ep).wait_recv()
 
     produced = dot(mid_all[...].reshape(128, HALF), down_vm[...])
     p9_send[...] = produced.astype(BF16).reshape(N_Y, 32, COLS)
-    p9_copy = y_copy(p9_send, p9_recv, p9_s, p9_r)
+    y_copy(p9_send, p9_recv, p9_s, p9_r, -1)
     back = p9_recv[...].reshape(128, COLS)
     to_tiles(dot(comb_scr[0], back) + dot(comb_scr[1], back), p10_send)
-    routed, p10_copy = z_scatter(p10_send, p10_recv, p10_s, p10_r)
+    routed = z_scatter(p10_send, 0, lambda step: N_Z - step, p10_recv, p10_s, p10_r)
     small_scr[...] = res_scr[...] + routed
     for j in range(NJ):
         layer_out[:, 128 * j : 128 * j + 128] = small_scr[4 * j : 4 * j + 4, :].astype(BF16)
 
-    each(N_CTX - 1, lambda i: p2_copy(i).wait_send())
-    each(N_Z - 1, lambda i: info_copy(i).wait_send())
-    each(N_Y - 1, lambda i: wo_copy(i).wait_send())
-    p3_each(lambda i: p3_copy(i).wait_send())
-    p4_sends(lambda i: p4_copy(i).wait_send())
-    each(N_Z - 1, lambda i: p5_copy(i).wait_send())
-    each(N_Z - 1, lambda i: p6_copy(i).wait_send())
-    each(N_Y - 1, lambda i: p6b_copy(i).wait_send())
-    each(N_CTX - 1, lambda i: p7_copy(i).wait_send())
-    each(N_CTX - 1, lambda i: p8_copy(i).wait_send())
-    each(N_Y - 1, lambda i: p9_copy(i).wait_send())
-    each(N_Z - 1, lambda i: p10_copy(i).wait_send())
+    finish()
 
 
 def per_device(
@@ -554,11 +570,17 @@
     w_up,
     w_down,
 ):
-    smem = pl.BlockSpec(memory_space=pltpu.SMEM)
     vmem = pl.BlockSpec(memory_space=pltpu.VMEM)
-    anywhere = pl.BlockSpec(memory_space=pl.ANY)
+    in_hbm = pl.BlockSpec(memory_space=pltpu.HBM)
     dma = pltpu.SemaphoreType.DMA
     scratch = [
+        pltpu.SMEM((4, 1, 4), jnp.int32),
+        pltpu.SMEM((4,), jnp.int32),
+        pltpu.SMEM((4, TOP), jnp.int32),
+        pltpu.SMEM((4, TOP), F32),
+        pltpu.VMEM((4, KDIM), BF16),
+        pltpu.VMEM((4, COLS), BF16),
+        pltpu.VMEM((COLS,), F32),
         pltpu.VMEM((4, 64, KDIM), BF16),
         pltpu.VMEM((1, 16, 64, KDIM), BF16),
         pltpu.VMEM((1, LAT, 128), BF16),
@@ -601,19 +623,19 @@
         pltpu.VMEM((N_Y, 32, COLS), BF16),
         pltpu.VMEM((N_Z, 32, 128), BF16),
         pltpu.VMEM((N_Z - 1, 32, 128), BF16),
-        dma((7,)),
+        dma((14,)),
     ]
-    for count in (3, 15, 7, 8, 8, 15, 15, 3, 7, 7, 3, 15):
-        scratch += [dma((count,)), dma((count,))]
+    for count in (3, 0, 0, 0, 8, 0, 0, 0, 0, 7, 0, 0):
+        scratch += [dma((count,)), dma((count,))] if count else [dma, dma]
     out = jax.ShapeDtypeStruct((4, COLS), BF16)
     return pl.pallas_call(
         kernel,
         out_shape=(out, out),
-        in_specs=[smem] * 4 + [vmem] * 3 + [anywhere] * 7,
+        in_specs=[in_hbm] * 14,
         out_specs=(vmem, vmem),
         scratch_shapes=scratch,
         compiler_params=pltpu.CompilerParams(
-            collective_id=0, has_side_effects=True, vmem_limit_bytes=40 * 1024 * 1024
+            collective_id=0, has_side_effects=True, vmem_limit_bytes=60 * 1024 * 1024
         ),
     )(
         page_table,
@@ -622,7 +644,7 @@
         route_weight,
         new_key,
         hidden_in,
-        norm_gain.reshape(1, COLS),
+        norm_gain,
         queries,
         latent_cache,
         w_uv,

time: 108 us -> 86.8 us (0.80)
  the two profiles are of different devices: /device:TPU:1 before, /device:TPU:6 now
where the time goes in v2:
time: 86.8 us; the launch traced here: 85.4 us
  Pallas kernels  82.2 us (95%)
  local copies, waits for them, and re-layouts  2.58 us (3%)
    pallas_call x1, Pallas kernels, per_device(): pl.pallas_call(kernel, out_shape=(out, out), in_specs=[in_hbm] * 14, out_...  82.2 us
    unnamed x2, local copies, waits for them, and re-layouts  2.58 us

profile of v2, /device:TPU:6, one launch (start us, length us, event | category | flops | bytes accessed | tf_op | source)
XLA Modules:
  0.0 85.4 jit_solution(16996090530085743454)
XLA Ops:
  0.6 82.2 %shard_map.149 = (bf16[4,896]{1,0:T(4,128)(2,1)}, bf16[4,896]{1,0:T(4,128)(2,1)}) custom-call(s32[4,1,4]{2,1,0:T(1,128)} %page_table_in.1, s32[4]{0:T(128)} %lengths_in.1, s32[4,8]{1,0:T(4,128)} %routes_in.1, f32[4,8]{1,0:T(4,128)} %route_weight_in.1, bf16[4,576]{1,0:T(4,128)(2,1)} %new_key_in.1, bf16[4,896]{1,0:T(4,128)(2,1)} %hidden_in.1, f32[896]{0:T(1024)} %gain_in.1, ...), custom_call_target="tpu_custom_call" | custom-call | tf_op jit(solution)/shard_map/pallas_call | solution.py:631
  82.8 1.3 %copy.18 = bf16[4,896]{1,0:T(4,128)(2,1)} copy(bf16[4,896]{1,0:T(4,128)(2,1)} %get-tuple-element.4) | data formatting | bytes 14336
  84.1 1.3 %copy.19 = bf16[4,896]{1,0:T(4,128)(2,1)} copy(bf16[4,896]{1,0:T(4,128)(2,1)} %get-tuple-element.5) | data formatting | bytes 14336

commit v3 on v2

--- a/solution.py
+++ b/solution.py
@@ -61,8 +61,7 @@
     w_gate,
     w_up,
     w_down,
-    attn_out,
-    layer_out,
+    out,
     page_table,
     lengths,
     routes,
@@ -127,6 +126,8 @@
     p5_r,
     p6_s,
     p6_r,
+    p6f_s,
+    p6f_r,
     p6b_s,
     p6b_r,
     p7_s,
@@ -144,6 +145,8 @@
     z = ep % N_Z
     g = ep // 8
     s8 = ep % 8
+    x = c // 2
+    core = c % 2
 
     def remote(src, dst, ssem, rsem, to_ctx, to_ep):
         return pltpu.make_async_remote_copy(
@@ -197,6 +200,14 @@
     def z_step(i):
         return 8 + (i + 1) // 2 * (1 - 2 * (i % 2))
 
+    def near(i):
+        step = z_step(8 + i)
+        return step, (step + 3 + step // 8) % N_Z
+
+    def far(i):
+        step = z_step(i)
+        return step, step + 4
+
     barrier = pltpu.get_barrier_semaphore()
 
     def greet(to_ctx, to_ep):
@@ -237,17 +248,15 @@
         before = before + named
     info = jnp.where(iota((32, 128), 1) < 64, pick, weight)
     info_send[...] = info.reshape(4, 8, 128)
-    info_recv[0] = info_send[z // 4]
-
-    small_scr[0:4, :] = jnp.zeros((4, 128), F32)
+    info_recv[7] = info_send[z // 4]
+
     hid_scr[28:32, :] = jnp.zeros((4, 128), F32)
-    gain_scr[28:32, :] = jnp.zeros((4, 128), F32)
+    gain_scr[...] = jnp.zeros((128, 128), F32)
     hid32 = hidden[...].astype(F32)
     for j in range(NJ):
         hid_scr[4 * j : 4 * j + 4, :] = hid32[:, 128 * j : 128 * j + 128]
-        gain_scr[4 * j : 4 * j + 4, :] = jnp.broadcast_to(
-            gain[128 * j : 128 * j + 128].reshape(1, 128), (4, 128)
-        )
+        gain_scr[j : j + 1, :] = gain[128 * j : 128 * j + 128].reshape(1, 128)
+    gain_scr[...] = jnp.transpose(gain_scr[...])
     nk_scr[...] = jnp.zeros((128, KDIM), BF16)
     nk_scr[0:4, :] = new_key[...]
     for zz in range(N_Z):
@@ -306,14 +315,15 @@
 
     ctx_scatter(p2_send, p2_recv, p2_s, p2_r)
 
-    def info_copy(i):
-        step = z_step(i)
+    def info_copy(i, place):
+        step, position = place(i)
         to = (z + step) % N_Z
         remote(
-            info_send.at[to // 4], info_recv.at[step], info_s, info_r, c, y * N_Z + to
+            info_send.at[to // 4], info_recv.at[position], info_s, info_r, c, y * N_Z + to
         ).start()
 
-    each(N_Z - 1, info_copy)
+    each(8, lambda i: info_copy(i, far))
+    each(7, lambda i: info_copy(i, near))
     pending.append(lambda: landed(info_recv.at[1:N_Z], info_s))
 
     for k in y_order:
@@ -355,6 +365,13 @@
         8, lambda i: remote(p3_send.at[i], p3_recv.at[s8], p3_s, p3_r, g_to, c * 8 + i).start()
     )
     pending.append(lambda: landed(p3_recv, p3_s))
+    loads[4].wait()
+    loads[5].wait()
+    for j in range(NJ):
+        factor = gain_scr[:, j : j + 1]
+        for w in (gate_vm, up_vm):
+            block = w[128 * j : 128 * j + 128, :].astype(F32)
+            w[128 * j : 128 * j + 128, :] = (block * factor).astype(BF16)
     loads[2].wait()
     landed(p3_recv, p3_r)
     tile_scr[...] = p3_recv[...].astype(F32).reshape(128, 128)
@@ -407,20 +424,28 @@
         p4_recv[slot4] = p4_send[...]
 
     landed(info_recv.at[1:N_Z], info_r)
-    for k in range(8):
-        col_scr[16 * k : 16 * k + 16, :] = info_recv[:, k, :]
+    for part in range(2):
+        for k in range(8):
+            row0 = 64 * part + 8 * k
+            col_scr[row0 : row0 + 8, :] = info_recv[8 * part : 8 * part + 8, k, :]
     pick_col = col_scr[:, 0:1].astype(jnp.int32)
     weight_col = col_scr[:, 64:65]
-    source = iota((128, 1), 0) % 16
+    source = iota((128, 1), 0) % 8
     target = source * 32 + pick_col
-    lane = iota((128, 512), 1)
-    for j in range(8):
-        sel_scr[128 * j : 128 * j + 128, :] = jnp.where(lane == target + 4 * j, 1.0, 0.0).astype(BF16)
+    lane = iota((64, 256), 1)
     spread = jnp.where(iota((128, 128), 1) == source * 4 + pick_col, weight_col, 0.0)
-    comb = jnp.transpose(spread)[0:64, :]
-    comb_hi = comb.astype(BF16)
-    comb_scr[0] = comb_hi
-    comb_scr[1] = (comb - comb_hi.astype(F32)).astype(BF16)
+    for part in range(2):
+        for j in range(NJ):
+            sel_scr[part, 64 * j : 64 * j + 64, :] = jnp.where(
+                lane == target[64 * part : 64 * part + 64] + 4 * j, 1.0, 0.0
+            ).astype(BF16)
+        block = jnp.concatenate(
+            [spread[64 * part : 64 * part + 64], jnp.zeros((64, 128), F32)], axis=0
+        )
+        comb = jnp.transpose(block)[0:32, :]
+        comb_hi = comb.astype(BF16)
+        comb_scr[part, 0] = comb_hi
+        comb_scr[part, 1] = (comb - comb_hi.astype(F32)).astype(BF16)
 
     loads[3].wait()
     for k in y_order:
@@ -430,92 +455,119 @@
         [p4_recv[2 * k : 2 * k + 2].reshape(64, 128) for k in range(N_Y)], axis=1
     )
 
-    def to_tiles(values32, send):
-        wide_scr[...] = values32
-        for zz in range(N_Z):
+    def to_tiles(values32, first, count):
+        wide_scr[0 : 4 * count, :] = values32
+        for zz in range(count):
             for j in range(NJ):
-                z_scr[32 * zz + 4 * j : 32 * zz + 4 * j + 4, :] = wide_scr[
+                row0 = 32 * (first + zz) + 4 * j
+                z_scr[row0 : row0 + 4, :] = wide_scr[
                     4 * zz : 4 * zz + 4, 128 * j : 128 * j + 128
                 ]
-        send[...] = z_scr[...].astype(BF16).reshape(N_Z, 32, 128)
-
-    def z_scatter(send, own, index, recv, ssem, rsem):
-        def copy(i):
-            step = z_step(i)
-            remote(
-                send.at[index(step)],
-                recv.at[step - 1],
-                ssem,
-                rsem,
-                c,
-                y * N_Z + (z + step) % N_Z,
-            ).start()
-
-        each(N_Z - 1, copy)
-        pending.append(lambda: landed(recv, ssem))
+        tiles = z_scr[32 * first : 32 * (first + count), :]
+        return tiles.astype(BF16).reshape(count, 32, 128)
+
+    def z_total(own, recv, rsem):
         total = z_scr[pl.ds(pl.multiple_of(own * 32, 32), 32), :]
         landed(recv, rsem)
         for i in range(N_Z - 1):
             total = total + recv[i].astype(F32)
         return total
 
-    to_tiles(dot(lhs, wout_vm[...].reshape(512, COLS)), p5_send)
-    attention = z_scatter(p5_send, z, lambda step: (z + step) % N_Z, p5_recv, p5_s, p5_r)
+    p5_send[...] = to_tiles(dot(lhs, wout_vm[...].reshape(512, COLS)), 0, N_Z)
+
+    def p5_copy(i):
+        step = z_step(i)
+        to = (z + step) % N_Z
+        remote(p5_send.at[to], p5_recv.at[step - 1], p5_s, p5_r, c, y * N_Z + to).start()
+
+    each(N_Z - 1, p5_copy)
+    pending.append(lambda: landed(p5_recv, p5_s))
+    attention = z_total(z, p5_recv, p5_r)
     residual = hid_scr[...] + attention
+    rounded = residual.astype(BF16)
+    p6_send[...] = rounded
+    p6_recv[7] = rounded
+
+    def p6_copy(i, place, ssem, rsem):
+        step, position = place(i)
+        remote(
+            p6_send, p6_recv.at[position], ssem, rsem, c, y * N_Z + (z + step) % N_Z
+        ).start()
+
+    each(8, lambda i: p6_copy(i, far, p6f_s, p6f_r))
+    each(7, lambda i: p6_copy(i, near, p6_s, p6_r))
+    pending.append(lambda: landed(p6_recv.at[0:7], p6_s))
+    pending.append(lambda: landed(p6_recv.at[8:16], p6f_s))
     res_scr[...] = residual
-    small_scr[...] = residual * residual
-    squares = small_scr[0:4, :]
-    for j in range(1, NJ):
-        squares = squares + small_scr[4 * j : 4 * j + 4, :]
-    squares = jnp.sum(squares, axis=1, keepdims=True)
-    small_scr[...] = residual * gain_scr[...]
-    small_scr[28:32, :] = three_parts(squares, (4, 128))
-    scaled = small_scr[...].astype(BF16)
-    p6_send[...] = scaled
-    p6_recv[0] = scaled
-
-    def p6_copy(i):
-        step = z_step(i)
-        remote(
-            p6_send, p6_recv.at[step], p6_s, p6_r, c, y * N_Z + (z + step) % N_Z
-        ).start()
-
-    each(N_Z - 1, p6_copy)
-    pending.append(lambda: landed(p6_recv.at[1:N_Z], p6_s))
     small_scr[...] = attention
     for j in range(NJ):
-        attn_out[:, 128 * j : 128 * j + 128] = small_scr[4 * j : 4 * j + 4, :].astype(BF16)
-    landed(p6_recv.at[1:N_Z], p6_r)
-
-    picked = dot(sel_scr[...], p6_recv[...].reshape(512, 128)).astype(BF16)
-    for j in range(8):
-        p6b_send[:, :, 128 * j : 128 * j + 128] = picked[128 * j : 128 * j + 128, :].reshape(
-            N_Y, 32, 128
-        )
-
-    def y_copy(send, recv, ssem, rsem, sign):
+        out[0:4, 128 * j : 128 * j + 128] = small_scr[4 * j : 4 * j + 4, :].astype(BF16)
+
+    def y_send(send, recv, ssem, rsem, sign):
         for k in y_order:
             remote(
                 send.at[k], recv.at[k], ssem, rsem, c, (y + N_Y + sign * k) % N_Y * N_Z + z
             ).start()
         pending.append(lambda: landed(recv.at[1:N_Y], ssem))
         recv[0] = send[0]
-        landed(recv.at[1:N_Y], rsem)
-
-    y_copy(p6b_send, xe, p6b_s, p6b_r, 1)
-
-    rows = xe[...].reshape(128, 1024)
-    loads[4].wait()
-    loads[5].wait()
-    p7_send[:, :, :HALF] = dot(rows[:, :COLS], gate_vm[...]).astype(BF16).reshape(N_CTX, 16, HALF)
-    p7_send[:, :, HALF : 2 * HALF] = (
-        dot(rows[:, :COLS], up_vm[...]).astype(BF16).reshape(N_CTX, 16, HALF)
-    )
-    p7_send[:, :, 2 * HALF :] = rows[:, COLS:].reshape(N_CTX, 16, 128)
-
-    ctx_scatter(p7_send, p7_recv, p7_s, p7_r)
+
+    def pick_rows(part):
+        arrived = p6_recv[8 * part : 8 * part + 8].reshape(256, 128)
+        picked = dot(sel_scr[part], arrived).astype(BF16)
+        for j in range(NJ):
+            p6b_send[part, :, :, 128 * j : 128 * j + 128] = picked[
+                64 * j : 64 * j + 64, :
+            ].reshape(N_Y, 16, 128)
+        y_send(p6b_send.at[part], xe.at[part], p6b_s.at[part], p6b_r.at[part], 1)
+
+    def gate_up(part):
+        landed(xe.at[part].at[1:N_Y], p6b_r.at[part])
+        rows = xe[part].reshape(64, COLS)
+        rows32 = rows.astype(F32)
+        squares = jnp.sum(rows32 * rows32, axis=1, keepdims=True)
+        p7_send[part, :, :, 2 * HALF :] = (
+            three_parts(squares, (64, 128)).astype(BF16).reshape(N_Y, 16, 128)
+        )
+        p7_send[part, :, :, :HALF] = dot(rows, gate_vm[...]).astype(BF16).reshape(N_Y, 16, HALF)
+        p7_send[part, :, :, HALF : 2 * HALF] = (
+            dot(rows, up_vm[...]).astype(BF16).reshape(N_Y, 16, HALF)
+        )
+        side = (core + part) % 2
+        for dx in (2, 1, 3):
+            there = (x + dx) % 4
+            remote(
+                p7_send.at[part, there],
+                p7_recv.at[2 * dx + side - 1],
+                p7_s.at[part],
+                p7_r,
+                there * 2 + part,
+                ep,
+            ).start()
+
+        @pl.when(core != part)
+        def _():
+            remote(
+                p7_send.at[part, x], p7_recv.at[0], p7_s.at[part], p7_r, x * 2 + part, ep
+            ).start()
+
+    def gate_up_sent(part):
+        landed(p7_recv.at[0:3], p7_s.at[part])
+
+        @pl.when(core != part)
+        def _():
+            landed(p7_recv.at[0], p7_s.at[part])
+
+    landed(p6_recv.at[0:7], p6_r)
+    pick_rows(0)
+    landed(p6_recv.at[8:16], p6f_r)
+    pick_rows(1)
+    gate_up(0)
+    gate_up(1)
+    pending.append(lambda: gate_up_sent(0))
+    pending.append(lambda: gate_up_sent(1))
+
     landed(p7_recv, p7_r)
-    sums = p7_send[c].astype(F32)
+    sums = p7_send[core, x].astype(F32)
     for i in range(N_CTX - 1):
         sums = sums + p7_recv[i].astype(F32)
     mean = jnp.sum(sums[:, 2 * HALF :], axis=1, keepdims=True) / D
@@ -524,32 +576,67 @@
     up = sums[:, HALF : 2 * HALF] * scale
     middle = (gate / (1.0 + jnp.exp(-gate)) * up).astype(BF16)
     p8_send[...] = middle
-    mid_all[c] = middle
-
+    mid_all[core, x] = middle
     for k in ctx_order:
         remote(
-            p8_send, mid_all.at[c], p8_s.at[k - 1], p8_r.at[k - 1], ctx_step(k), ep
+            p8_send, mid_all.at[core, x], p8_s.at[k - 1], p8_r.at[k - 1], ctx_step(k), ep
         ).start()
     for k in ctx_order:
         pending.append(
             remote(
-                p8_send, mid_all.at[c], p8_s.at[k - 1], p8_r.at[k - 1], ctx_step(k), ep
+                p8_send, mid_all.at[core, x], p8_s.at[k - 1], p8_r.at[k - 1], ctx_step(k), ep
             ).wait_send
         )
     loads[6].wait()
-    for k in ctx_order:
-        frm = ctx_back(k)
-        remote(p8_send, mid_all.at[frm], p8_s.at[k - 1], p8_r.at[k - 1], frm, ep).wait_recv()
-
-    produced = dot(mid_all[...].reshape(128, HALF), down_vm[...])
-    p9_send[...] = produced.astype(BF16).reshape(N_Y, 32, COLS)
-    y_copy(p9_send, p9_recv, p9_s, p9_r, -1)
-    back = p9_recv[...].reshape(128, COLS)
-    to_tiles(dot(comb_scr[0], back) + dot(comb_scr[1], back), p10_send)
-    routed = z_scatter(p10_send, 0, lambda step: N_Z - step, p10_recv, p10_s, p10_r)
+
+    def project(part):
+        side = (core + part) % 2
+        for dx in (1, 3, 2):
+            frm = (x + 4 - dx) % 4
+            sem = 2 * dx + side - 1
+            remote(
+                p8_send, mid_all.at[part, frm], p8_s.at[sem], p8_r.at[sem], frm * 2 + part, ep
+            ).wait_recv()
+
+        @pl.when(core != part)
+        def _():
+            remote(
+                p8_send, mid_all.at[part, x], p8_s.at[0], p8_r.at[0], x * 2 + part, ep
+            ).wait_recv()
+
+        produced = dot(mid_all[part].reshape(64, HALF), down_vm[...])
+        p9_send[part] = produced.astype(BF16).reshape(N_Y, 16, COLS)
+        y_send(p9_send.at[part], p9_recv.at[part], p9_s.at[part], p9_r.at[part], -1)
+
+    project(0)
+    project(1)
+
+    def combine(part, count, place):
+        landed(p9_recv.at[part].at[1:N_Y], p9_r.at[part])
+        back = p9_recv[part].reshape(64, COLS)
+        mixed = dot(comb_scr[part, 0][:, :64], back) + dot(comb_scr[part, 1][:, :64], back)
+        p10_send[8 * part : 8 * part + 8] = to_tiles(mixed, 8 * part, 8)
+
+        def copy(i):
+            step, position = place(i)
+            remote(
+                p10_send.at[position],
+                p10_recv.at[step - 1],
+                p10_s,
+                p10_r,
+                c,
+                y * N_Z + (z + N_Z - step) % N_Z,
+            ).start()
+
+        each(count, copy)
+
+    combine(0, 7, near)
+    combine(1, 8, far)
+    pending.append(lambda: landed(p10_recv, p10_s))
+    routed = z_total(7, p10_recv, p10_r)
     small_scr[...] = res_scr[...] + routed
     for j in range(NJ):
-        layer_out[:, 128 * j : 128 * j + 128] = small_scr[4 * j : 4 * j + 4, :].astype(BF16)
+        out[4:8, 128 * j : 128 * j + 128] = small_scr[4 * j : 4 * j + 4, :].astype(BF16)
 
     finish()
 
@@ -596,11 +683,11 @@
         pltpu.VMEM((512, 128), F32),
         pltpu.VMEM((32, 128), F32),
         pltpu.VMEM((32, 128), F32),
-        pltpu.VMEM((32, 128), F32),
+        pltpu.VMEM((128, 128), F32),
         pltpu.VMEM((32, 128), F32),
         pltpu.VMEM((128, 128), F32),
-        pltpu.VMEM((1024, 512), BF16),
-        pltpu.VMEM((2, 64, 128), BF16),
+        pltpu.VMEM((2, 64 * NJ, 256), BF16),
+        pltpu.VMEM((2, 2, 32, 128), BF16),
         pltpu.VMEM((4, 8, 128), F32),
         pltpu.VMEM((N_Z, 8, 128), F32),
         pltpu.VMEM((N_CTX, 32, 640), BF16),
@@ -613,26 +700,28 @@
         pltpu.VMEM((N_Z - 1, 32, 128), BF16),
         pltpu.VMEM((32, 128), BF16),
         pltpu.VMEM((N_Z, 32, 128), BF16),
-        pltpu.VMEM((N_Y, 32, 1024), BF16),
-        pltpu.VMEM((N_Y, 32, 1024), BF16),
-        pltpu.VMEM((N_CTX, 16, 1152), BF16),
+        pltpu.VMEM((2, N_Y, 16, COLS), BF16),
+        pltpu.VMEM((2, N_Y, 16, COLS), BF16),
+        pltpu.VMEM((2, 4, 16, 1152), BF16),
         pltpu.VMEM((N_CTX - 1, 16, 1152), BF16),
         pltpu.VMEM((16, HALF), BF16),
-        pltpu.VMEM((N_CTX, 16, HALF), BF16),
-        pltpu.VMEM((N_Y, 32, COLS), BF16),
-        pltpu.VMEM((N_Y, 32, COLS), BF16),
+        pltpu.VMEM((2, 4, 16, HALF), BF16),
+        pltpu.VMEM((2, N_Y, 16, COLS), BF16),
+        pltpu.VMEM((2, N_Y, 16, COLS), BF16),
         pltpu.VMEM((N_Z, 32, 128), BF16),
         pltpu.VMEM((N_Z - 1, 32, 128), BF16),
         dma((14,)),
     ]
-    for count in (3, 0, 0, 0, 8, 0, 0, 0, 0, 7, 0, 0):
+    for count in (3, 0, 0, 0, 8, 0, 0, 0, 2):
         scratch += [dma((count,)), dma((count,))] if count else [dma, dma]
-    out = jax.ShapeDtypeStruct((4, COLS), BF16)
-    return pl.pallas_call(
+    scratch += [dma((2,)), dma]
+    for count in (7, 2, 0):
+        scratch += [dma((count,)), dma((count,))] if count else [dma, dma]
+    both = pl.pallas_call(
         kernel,
-        out_shape=(out, out),
+        out_shape=jax.ShapeDtypeStruct((8, COLS), BF16),
         in_specs=[in_hbm] * 14,
-        out_specs=(vmem, vmem),
+        out_specs=vmem,
         scratch_shapes=scratch,
         compiler_params=pltpu.CompilerParams(
             collective_id=0, has_side_effects=True, vmem_limit_bytes=60 * 1024 * 1024
@@ -653,6 +742,7 @@
         w_up,
         w_down,
     )
+    return both[:4], both[4:]
 
 
 def solution(mesh):

time: 86.8 us -> 83.8 us (0.965)
  Pallas kernels: 82.2 us -> 80.6 us
  local copies, waits for them, and re-layouts: 2.58 us -> 1.39 us
    unnamed x2 -> x0, local copies, waits for them, and re-layouts: 2.58 us -> none
    pallas_call x1, Pallas kernels: 82.2 us -> 80.6 us  [per_device(): pl.pallas_call(kernel, out_shape=jax.ShapeDtypeStruct((8, COLS), BF16), i...]
    slice x0 -> x1, local copies, waits for them, and re-layouts: none -> 1.39 us  [per_device(): return (both[:4], both[4:])]
where the time goes in v3:
time: 83.8 us; the launch traced here: 82.6 us
  Pallas kernels  80.6 us (96%)
  local copies, waits for them, and re-layouts  1.39 us (2%)
    pallas_call x1, Pallas kernels, per_device(): pl.pallas_call(kernel, out_shape=jax.ShapeDtypeStruct((8, COLS), BF16), i...  80.6 us

profile of v3, /device:TPU:6, one launch (start us, length us, event | category | flops | bytes accessed | tf_op | source)
XLA Modules:
  0.0 82.6 jit_solution(398504863146512258)
XLA Ops:
  0.6 80.6 %shard_map.149 = bf16[8,896]{1,0:T(8,128)(2,1)} custom-call(s32[4,1,4]{2,1,0:T(1,128)} %page_table_in.1, s32[4]{0:T(128)} %lengths_in.1, s32[4,8]{1,0:T(4,128)} %routes_in.1, f32[4,8]{1,0:T(4,128)} %route_weight_in.1, bf16[4,576]{1,0:T(4,128)(2,1)} %new_key_in.1, bf16[4,896]{1,0:T(4,128)(2,1)} %hidden_in.1, f32[896]{0:T(1024)} %gain_in.1, ...), custom_call_target="tpu_custom_call" | custom-call | tf_op jit(solution)/shard_map/pallas_call | solution.py:720
  81.2 1.4 %fusion = (bf16[4,896]{1,0:T(4,128)(2,1)}, bf16[4,896]{1,0:T(4,128)(2,1)}) fusion(bf16[8,896]{1,0:T(8,128)(2,1)} %shard_map.149), kind=kLoop, calls=%fused_computation | loop fusion | bytes 28672 | tf_op jit(solution)/shard_map/slice | solution.py:745

commit v4 on v3

--- a/solution.py
+++ b/solution.py
@@ -112,6 +112,8 @@
     p10_send,
     p10_recv,
     lsem,
+    uv_s,
+    uv_r,
     wo_s,
     wo_r,
     info_s,
@@ -143,10 +145,9 @@
     ep = lax.axis_index("ep")
     y = ep // N_Z
     z = ep % N_Z
-    g = ep // 8
-    s8 = ep % 8
     x = c // 2
     core = c % 2
+    has_head = z // 8 == core
 
     def remote(src, dst, ssem, rsem, to_ctx, to_ep):
         return pltpu.make_async_remote_copy(
@@ -171,7 +172,7 @@
             [
                 (queries, q_vm),
                 (cache, cache_vm),
-                (w_uv, wuv_vm),
+                (w_uv, wuv_vm.at[0:1]),
                 (w_out, wout_vm.at[y]),
                 (w_gate, gate_vm),
                 (w_up, up_vm),
@@ -215,16 +216,9 @@
             barrier, inc=1, device_id={"ctx": to_ctx, "ep": to_ep}, device_id_type=MESH
         )
 
-    def greet_plane(i):
-        k = i + 1
-        greet((c + k % N_CTX) % N_CTX, (y + k // N_CTX) % N_Y * N_Z + z)
-
-    g_to = (g + 4) % 8
-    c_from = (c + 4) % 8
     each(N_Z - 1, lambda i: greet(c, y * N_Z + (z + z_step(i)) % N_Z))
-    each(8, lambda i: greet(g_to, c * 8 + i))
-    each(8, lambda i: greet(g, c_from * 8 + i))
-    each(N_CTX * N_Y - 1, greet_plane)
+    each(N_Y - 1, lambda i: greet(c, (y + i + 1) % N_Y * N_Z + z))
+    each(N_CTX - 1, lambda i: greet((c + i + 1) % N_CTX, ep))
 
     for load in loads[7:]:
         load.wait()
@@ -296,7 +290,7 @@
     p2_send[:, :, :LAT] = (mixture / total).astype(BF16).reshape(N_CTX, 32, LAT)
     p2_send[:, :, LAT:] = three_parts(logsum, (256, 128)).astype(BF16).reshape(N_CTX, 32, 128)
 
-    pl.semaphore_wait(barrier, N_CTX * N_Y - 1 + N_Z - 1 + 16)
+    pl.semaphore_wait(barrier, N_Z - 1 + N_Y - 1 + N_CTX - 1)
 
     def ctx_step(k):
         return (c // 2 + k // 2) % 4 * 2 + (c + k) % 2
@@ -325,6 +319,29 @@
     each(8, lambda i: info_copy(i, far))
     each(7, lambda i: info_copy(i, near))
     pending.append(lambda: landed(info_recv.at[1:N_Z], info_s))
+
+    def uv_copy(k):
+        return remote(
+            w_uv,
+            wuv_vm.at[1:2],
+            uv_s.at[k - 1],
+            uv_r,
+            c,
+            (y + k) % N_Y * N_Z + z,
+        )
+
+    @pl.when(has_head & (y == x))
+    def _():
+        for k in y_order:
+            uv_copy(k).start()
+
+    def uv_sent():
+        @pl.when(has_head & (y == x))
+        def _():
+            for k in y_order:
+                uv_copy(k).wait_send()
+
+    pending.append(uv_sent)
 
     for k in y_order:
         remote(
@@ -359,12 +376,32 @@
             tile_scr[16 * i + 4 * j : 16 * i + 4 * j + 4, :] = att_scr[
                 4 * i : 4 * i + 4, 128 * j : 128 * j + 128
             ]
-    p3_send[...] = tile_scr[...].astype(BF16).reshape(8, 16, 128)
-
-    each(
-        8, lambda i: remote(p3_send.at[i], p3_recv.at[s8], p3_s, p3_r, g_to, c * 8 + i).start()
+    p3_send[...] = tile_scr[0:128, :].astype(BF16).reshape(8, 16, 128)
+
+    def p3_each(step):
+        def one(i):
+            @pl.when(z != 8 * core + i)
+            def _():
+                step(i)
+
+        each(8, one)
+
+    p3_each(
+        lambda i: remote(
+            p3_send.at[i], p3_recv.at[z], p3_s, p3_r, c, y * N_Z + 8 * core + i
+        ).start()
     )
-    pending.append(lambda: landed(p3_recv, p3_s))
+
+    def p3_sent():
+        @pl.when(has_head)
+        def _():
+            landed(p3_send.at[0:7], p3_s)
+
+        @pl.when(jnp.logical_not(has_head))
+        def _():
+            landed(p3_send, p3_s)
+
+    pending.append(p3_sent)
     loads[4].wait()
     loads[5].wait()
     for j in range(NJ):
@@ -373,55 +410,40 @@
             block = w[128 * j : 128 * j + 128, :].astype(F32)
             w[128 * j : 128 * j + 128, :] = (block * factor).astype(BF16)
     loads[2].wait()
-    landed(p3_recv, p3_r)
-    tile_scr[...] = p3_recv[...].astype(F32).reshape(128, 128)
-    for i in range(8):
-        for j in range(4):
-            lhs_scr[4 * i : 4 * i + 4, 128 * j : 128 * j + 128] = tile_scr[
-                16 * i + 4 * j : 16 * i + 4 * j + 4, :
-            ]
-    values = dot(lhs_scr[...].astype(BF16), wuv_vm[0]).astype(BF16)
-    p4_send[...] = values
-
-    home = (c // 2 + 2) % N_Y
-    mine = home == y
-    slot4 = y * 2 + c % 2
-
-    def p4_copy(i):
-        return remote(p4_send, p4_recv.at[slot4], p4_s.at[i], p4_r.at[slot4], i, home * N_Z + z)
-
-    def p4_arrival(i):
-        return remote(
-            p4_send,
-            p4_recv.at[i],
-            p4_s.at[i],
-            p4_r.at[i],
-            (y + 2) % N_Y * 2 + i % 2,
-            i // 2 * N_Z + z,
-        )
-
-    def p4_sends(step):
-        def one(i):
-            @pl.when(jnp.logical_not(mine & (i == c)))
-            def _():
-                step(i)
-
-        each(8, one)
-
-    def p4_arrives(step):
-        def one(i):
-            @pl.when(jnp.logical_not(mine & (i == slot4)))
-            def _():
-                step(i)
-
-        each(8, one)
-
-    p4_sends(lambda i: p4_copy(i).start())
-    pending.append(lambda: p4_sends(lambda i: p4_copy(i).wait_send()))
-
-    @pl.when(mine)
+
+    def p4_copy(k):
+        return remote(p4_send, p4_recv.at[x], p4_s.at[k - 1], p4_r, ctx_step(k), ep)
+
+    @pl.when(has_head)
     def _():
-        p4_recv[slot4] = p4_send[...]
+        p3_recv[z] = p3_send[z % 8]
+        landed(p3_recv.at[1:N_Z], p3_r)
+
+        @pl.when(y != x)
+        def _():
+            remote(w_uv, wuv_vm.at[1:2], uv_s.at[0], uv_r, c, x * N_Z + z).wait_recv()
+
+        tile_scr[...] = p3_recv[...].astype(F32).reshape(256, 128)
+        for i in range(N_Z):
+            for j in range(4):
+                lhs_scr[4 * i : 4 * i + 4, 128 * j : 128 * j + 128] = tile_scr[
+                    16 * i + 4 * j : 16 * i + 4 * j + 4, :
+                ]
+        which = jnp.where(y == x, 0, 1).astype(jnp.int32)
+        values = dot(lhs_scr[...].astype(BF16), wuv_vm[which]).astype(BF16)
+        p4_send[...] = values
+        p4_recv[x] = values
+
+        for k in ctx_order:
+            p4_copy(k).start()
+
+    def p4_sent():
+        @pl.when(has_head)
+        def _():
+            for k in ctx_order:
+                p4_copy(k).wait_send()
+
+    pending.append(p4_sent)
 
     landed(info_recv.at[1:N_Z], info_r)
     for part in range(2):
@@ -450,10 +472,15 @@
     loads[3].wait()
     for k in y_order:
         wo_arrival(k).wait_recv()
-    p4_arrives(lambda i: p4_arrival(i).wait_recv())
-    lhs = jnp.concatenate(
-        [p4_recv[2 * k : 2 * k + 2].reshape(64, 128) for k in range(N_Y)], axis=1
-    )
+    @pl.when(has_head)
+    def _():
+        landed(p4_recv.at[0:3], p4_r)
+
+    @pl.when(jnp.logical_not(has_head))
+    def _():
+        landed(p4_recv, p4_r)
+
+    lhs = jnp.concatenate([p4_recv[k] for k in range(N_Y)], axis=1)
 
     def to_tiles(values32, first, count):
         wide_scr[0 : 4 * count, :] = values32
@@ -494,8 +521,8 @@
             p6_send, p6_recv.at[position], ssem, rsem, c, y * N_Z + (z + step) % N_Z
         ).start()
 
+    each(7, lambda i: p6_copy(i, near, p6_s, p6_r))
     each(8, lambda i: p6_copy(i, far, p6f_s, p6f_r))
-    each(7, lambda i: p6_copy(i, near, p6_s, p6_r))
     pending.append(lambda: landed(p6_recv.at[0:7], p6_s))
     pending.append(lambda: landed(p6_recv.at[8:16], p6f_s))
     res_scr[...] = residual
@@ -608,8 +635,8 @@
         p9_send[part] = produced.astype(BF16).reshape(N_Y, 16, COLS)
         y_send(p9_send.at[part], p9_recv.at[part], p9_s.at[part], p9_r.at[part], -1)
 
+    project(1)
     project(0)
-    project(1)
 
     def combine(part, count, place):
         landed(p9_recv.at[part].at[1:N_Y], p9_r.at[part])
@@ -630,8 +657,8 @@
 
         each(count, copy)
 
+    combine(1, 8, far)
     combine(0, 7, near)
-    combine(1, 8, far)
     pending.append(lambda: landed(p10_recv, p10_s))
     routed = z_total(7, p10_recv, p10_r)
     small_scr[...] = res_scr[...] + routed
@@ -670,15 +697,15 @@
         pltpu.VMEM((COLS,), F32),
         pltpu.VMEM((4, 64, KDIM), BF16),
         pltpu.VMEM((1, 16, 64, KDIM), BF16),
-        pltpu.VMEM((1, LAT, 128), BF16),
+        pltpu.VMEM((2, LAT, 128), BF16),
         pltpu.VMEM((N_Y, 128, COLS), BF16),
         pltpu.VMEM((COLS, HALF), BF16),
         pltpu.VMEM((COLS, HALF), BF16),
         pltpu.VMEM((HALF, COLS), BF16),
         pltpu.VMEM((128, KDIM), BF16),
         pltpu.VMEM((32, LAT), F32),
-        pltpu.VMEM((128, 128), F32),
-        pltpu.VMEM((32, LAT), F32),
+        pltpu.VMEM((256, 128), F32),
+        pltpu.VMEM((64, LAT), F32),
         pltpu.VMEM((64, COLS), F32),
         pltpu.VMEM((512, 128), F32),
         pltpu.VMEM((32, 128), F32),
@@ -693,9 +720,9 @@
         pltpu.VMEM((N_CTX, 32, 640), BF16),
         pltpu.VMEM((N_CTX - 1, 32, 640), BF16),
         pltpu.VMEM((8, 16, 128), BF16),
-        pltpu.VMEM((8, 16, 128), BF16),
-        pltpu.VMEM((32, 128), BF16),
-        pltpu.VMEM((8, 32, 128), BF16),
+        pltpu.VMEM((N_Z, 16, 128), BF16),
+        pltpu.VMEM((64, 128), BF16),
+        pltpu.VMEM((N_Y, 64, 128), BF16),
         pltpu.VMEM((N_Z, 32, 128), BF16),
         pltpu.VMEM((N_Z - 1, 32, 128), BF16),
         pltpu.VMEM((32, 128), BF16),
@@ -712,8 +739,9 @@
         pltpu.VMEM((N_Z - 1, 32, 128), BF16),
         dma((14,)),
     ]
-    for count in (3, 0, 0, 0, 8, 0, 0, 0, 2):
-        scratch += [dma((count,)), dma((count,))] if count else [dma, dma]
+    scratch += [dma((3,)), dma]
+    scratch += [dma((3,)), dma((3,))] + [dma] * 6 + [dma((7,)), dma] + [dma] * 6
+    scratch += [dma((2,)), dma((2,))]
     scratch += [dma((2,)), dma]
     for count in (7, 2, 0):
         scratch += [dma((count,)), dma((count,))] if count else [dma, dma]

time: 83.8 us -> 79 us (0.943)
  the two profiles are of different devices: /device:TPU:6 before, /device:TPU:32 now
where the time goes in v4:
time: 79 us; the launch traced here: 78.8 us
  Pallas kernels  76.7 us (97%)
  local copies, waits for them, and re-layouts  1.39 us (2%)
    pallas_call x1, Pallas kernels, per_device(): pl.pallas_call(kernel, out_shape=jax.ShapeDtypeStruct((8, COLS), BF16), i...  76.7 us

profile of v4, /device:TPU:32, one launch (start us, length us, event | category | flops | bytes accessed | tf_op | source)
XLA Modules:
  0.0 78.8 jit_solution(14377387076598127446)
XLA Ops:
  0.6 76.7 %shard_map.149 = bf16[8,896]{1,0:T(8,128)(2,1)} custom-call(s32[4,1,4]{2,1,0:T(1,128)} %page_table_in.1, s32[4]{0:T(128)} %lengths_in.1, s32[4,8]{1,0:T(4,128)} %routes_in.1, f32[4,8]{1,0:T(4,128)} %route_weight_in.1, bf16[4,576]{1,0:T(4,128)(2,1)} %new_key_in.1, bf16[4,896]{1,0:T(4,128)(2,1)} %hidden_in.1, f32[896]{0:T(1024)} %gain_in.1, ...), custom_call_target="tpu_custom_call" | custom-call | tf_op jit(solution)/shard_map/pallas_call | solution.py:748
  77.4 1.4 %fusion = (bf16[4,896]{1,0:T(4,128)(2,1)}, bf16[4,896]{1,0:T(4,128)(2,1)}) fusion(bf16[8,896]{1,0:T(8,128)(2,1)} %shard_map.149), kind=kLoop, calls=%fused_computation | loop fusion | bytes 28672 | tf_op jit(solution)/shard_map/slice | solution.py:773

commit v5 on v4

--- a/solution.py
+++ b/solution.py
@@ -203,7 +203,7 @@
 
     def near(i):
         step = z_step(8 + i)
-        return step, (step + 3 + step // 8) % N_Z
+        return step, step % 8
 
     def far(i):
         step = z_step(i)
@@ -242,7 +242,7 @@
         before = before + named
     info = jnp.where(iota((32, 128), 1) < 64, pick, weight)
     info_send[...] = info.reshape(4, 8, 128)
-    info_recv[7] = info_send[z // 4]
+    info_recv[0] = info_send[z // 4]
 
     hid_scr[28:32, :] = jnp.zeros((4, 128), F32)
     gain_scr[...] = jnp.zeros((128, 128), F32)
@@ -379,18 +379,22 @@
     p3_send[...] = tile_scr[0:128, :].astype(BF16).reshape(8, 16, 128)
 
     def p3_each(step):
-        def one(i):
+        def one(n):
+            i = (z + z_step(n)) % 8
+
             @pl.when(z != 8 * core + i)
             def _():
                 step(i)
 
         each(8, one)
 
-    p3_each(
-        lambda i: remote(
-            p3_send.at[i], p3_recv.at[z], p3_s, p3_r, c, y * N_Z + 8 * core + i
+    def p3_copy(i):
+        to = 8 * core + i
+        remote(
+            p3_send.at[i], p3_recv.at[(to + N_Z - z) % N_Z], p3_s, p3_r, c, y * N_Z + to
         ).start()
-    )
+
+    p3_each(p3_copy)
 
     def p3_sent():
         @pl.when(has_head)
@@ -416,7 +420,7 @@
 
     @pl.when(has_head)
     def _():
-        p3_recv[z] = p3_send[z % 8]
+        p3_recv[0] = p3_send[z % 8]
         landed(p3_recv.at[1:N_Z], p3_r)
 
         @pl.when(y != x)
@@ -493,27 +497,40 @@
         tiles = z_scr[32 * first : 32 * (first + count), :]
         return tiles.astype(BF16).reshape(count, 32, 128)
 
-    def z_total(own, recv, rsem):
-        total = z_scr[pl.ds(pl.multiple_of(own * 32, 32), 32), :]
+    def z_send(values32, part, send, recv, ssem, rsem):
+        send[8 * part : 8 * part + 8] = to_tiles(values32, 8 * part, 8)
+        count, place = ((7, near), (8, far))[part]
+
+        def copy(i):
+            step, position = place(i)
+            remote(
+                send.at[position],
+                recv.at[step - 1],
+                ssem,
+                rsem,
+                c,
+                y * N_Z + (z + N_Z - step) % N_Z,
+            ).start()
+
+        each(count, copy)
+
+    def z_total(recv, rsem):
+        total = z_scr[0:32, :]
         landed(recv, rsem)
         for i in range(N_Z - 1):
             total = total + recv[i].astype(F32)
         return total
 
-    p5_send[...] = to_tiles(dot(lhs, wout_vm[...].reshape(512, COLS)), 0, N_Z)
-
-    def p5_copy(i):
-        step = z_step(i)
-        to = (z + step) % N_Z
-        remote(p5_send.at[to], p5_recv.at[step - 1], p5_s, p5_r, c, y * N_Z + to).start()
-
-    each(N_Z - 1, p5_copy)
+    projection = wout_vm[...].reshape(512, COLS)
+    z_send(dot(lhs[16:48], projection), 1, p5_send, p5_recv, p5_s, p5_r)
+    others = jnp.concatenate([lhs[0:16], lhs[48:64]], axis=0)
+    z_send(dot(others, projection), 0, p5_send, p5_recv, p5_s, p5_r)
     pending.append(lambda: landed(p5_recv, p5_s))
-    attention = z_total(z, p5_recv, p5_r)
+    attention = z_total(p5_recv, p5_r)
     residual = hid_scr[...] + attention
     rounded = residual.astype(BF16)
     p6_send[...] = rounded
-    p6_recv[7] = rounded
+    p6_recv[0] = rounded
 
     def p6_copy(i, place, ssem, rsem):
         step, position = place(i)
@@ -521,9 +538,9 @@
             p6_send, p6_recv.at[position], ssem, rsem, c, y * N_Z + (z + step) % N_Z
         ).start()
 
+    each(8, lambda i: p6_copy(i, far, p6f_s, p6f_r))
     each(7, lambda i: p6_copy(i, near, p6_s, p6_r))
-    each(8, lambda i: p6_copy(i, far, p6f_s, p6f_r))
-    pending.append(lambda: landed(p6_recv.at[0:7], p6_s))
+    pending.append(lambda: landed(p6_recv.at[1:8], p6_s))
     pending.append(lambda: landed(p6_recv.at[8:16], p6f_s))
     res_scr[...] = residual
     small_scr[...] = attention
@@ -584,7 +601,7 @@
         def _():
             landed(p7_recv.at[0], p7_s.at[part])
 
-    landed(p6_recv.at[0:7], p6_r)
+    landed(p6_recv.at[1:8], p6_r)
     pick_rows(0)
     landed(p6_recv.at[8:16], p6f_r)
     pick_rows(1)
@@ -638,34 +655,20 @@
     project(1)
     project(0)
 
-    def combine(part, count, place):
+    def combine(part):
         landed(p9_recv.at[part].at[1:N_Y], p9_r.at[part])
         back = p9_recv[part].reshape(64, COLS)
         mixed = dot(comb_scr[part, 0][:, :64], back) + dot(comb_scr[part, 1][:, :64], back)
-        p10_send[8 * part : 8 * part + 8] = to_tiles(mixed, 8 * part, 8)
-
-        def copy(i):
-            step, position = place(i)
-            remote(
-                p10_send.at[position],
-                p10_recv.at[step - 1],
-                p10_s,
-                p10_r,
-                c,
-                y * N_Z + (z + N_Z - step) % N_Z,
-            ).start()
-
-        each(count, copy)
-
-    combine(1, 8, far)
-    combine(0, 7, near)
-    pending.append(lambda: landed(p10_recv, p10_s))
-    routed = z_total(7, p10_recv, p10_r)
+        z_send(mixed, part, p10_send, p10_recv, p10_s, p10_r)
+
+    combine(1)
+    combine(0)
+    finish()
+    routed = z_total(p10_recv, p10_r)
+    landed(p10_recv, p10_s)
     small_scr[...] = res_scr[...] + routed
     for j in range(NJ):
         out[4:8, 128 * j : 128 * j + 128] = small_scr[4 * j : 4 * j + 4, :].astype(BF16)
-
-    finish()
 
 
 def per_device(

time: 79 us -> 76.3 us (0.966)
  the two profiles are of different devices: /device:TPU:32 before, /device:TPU:6 now
where the time goes in v5:
time: 76.3 us; the launch traced here: 76.1 us
  Pallas kernels  74 us (97%)
  local copies, waits for them, and re-layouts  1.39 us (2%)
    pallas_call x1, Pallas kernels, per_device(): pl.pallas_call(kernel, out_shape=jax.ShapeDtypeStruct((8, COLS), BF16), i...  74 us

profile of v5, /device:TPU:6, one launch (start us, length us, event | category | flops | bytes accessed | tf_op | source)
XLA Modules:
  0.0 76.1 jit_solution(14880881659174174691)
XLA Ops:
  0.6 74.0 %shard_map.149 = bf16[8,896]{1,0:T(8,128)(2,1)} custom-call(s32[4,1,4]{2,1,0:T(1,128)} %page_table_in.1, s32[4]{0:T(128)} %lengths_in.1, s32[4,8]{1,0:T(4,128)} %routes_in.1, f32[4,8]{1,0:T(4,128)} %route_weight_in.1, bf16[4,576]{1,0:T(4,128)(2,1)} %new_key_in.1, bf16[4,896]{1,0:T(4,128)(2,1)} %hidden_in.1, f32[896]{0:T(1024)} %gain_in.1, ...), custom_call_target="tpu_custom_call" | custom-call | tf_op jit(solution)/shard_map/pallas_call | solution.py:751
  74.7 1.4 %fusion = (bf16[4,896]{1,0:T(4,128)(2,1)}, bf16[4,896]{1,0:T(4,128)(2,1)}) fusion(bf16[8,896]{1,0:T(8,128)(2,1)} %shard_map.149), kind=kLoop, calls=%fused_computation | loop fusion | bytes 28672 | tf_op jit(solution)/shard_map/slice | solution.py:776

commit v6 on v5

--- a/solution.py
+++ b/solution.py
@@ -105,6 +105,8 @@
     xe,
     p7_send,
     p7_recv,
+    p7u_send,
+    p7u_recv,
     p8_send,
     mid_all,
     p9_send,
@@ -134,6 +136,8 @@
     p6b_r,
     p7_s,
     p7_r,
+    p7u_s,
+    p7u_r,
     p8_s,
     p8_r,
     p9_s,
@@ -287,8 +291,15 @@
     some = total > 0.0
     total = jnp.where(some, total, 1.0)
     logsum = jnp.where(some, peak + jnp.log(total), very_low)
-    p2_send[:, :, :LAT] = (mixture / total).astype(BF16).reshape(N_CTX, 32, LAT)
-    p2_send[:, :, LAT:] = three_parts(logsum, (256, 128)).astype(BF16).reshape(N_CTX, 32, 128)
+    mixture = (mixture / total).astype(BF16)
+    for j in range(4):
+        p2_send[:, 32 * j : 32 * j + 32, :] = mixture[:, 128 * j : 128 * j + 128].reshape(
+            N_CTX, 32, 128
+        )
+    logsum = three_parts(logsum, (256, 128)).reshape(N_CTX, 32, 128)
+    p2_send[:, 128:144, :] = jnp.where(
+        iota((N_CTX, 16, 128), 2) < 64, logsum[:, :16], jnp.roll(logsum[:, 16:], 64, axis=2)
+    ).astype(BF16)
 
     pl.semaphore_wait(barrier, N_Z - 1 + N_Y - 1 + N_CTX - 1)
 
@@ -360,17 +371,30 @@
 
     landed(p2_recv, p2_r)
     parts = [p2_send[c]] + [p2_recv[i] for i in range(N_CTX - 1)]
-    logs = [jnp.sum(p[:, LAT:].astype(F32), axis=1, keepdims=True) for p in parts]
+    def row_logs(p):
+        both = p[128:144].astype(F32)
+        first = iota((16, 128), 1) < 64
+        return jnp.concatenate(
+            [
+                jnp.sum(jnp.where(first, both, 0.0), axis=1, keepdims=True),
+                jnp.sum(jnp.where(first, 0.0, both), axis=1, keepdims=True),
+            ],
+            axis=0,
+        )
+
+    logs = [row_logs(p) for p in parts]
     top = logs[0]
     for l in logs[1:]:
         top = jnp.maximum(top, l)
-    above = jnp.zeros((32, LAT), F32)
-    below = jnp.zeros((32, 1), F32)
-    for p, l in zip(parts, logs):
-        f = jnp.exp(l - top)
-        above = above + f * p[:, :LAT].astype(F32)
+    factors = [jnp.exp(l - top) for l in logs]
+    below = factors[0]
+    for f in factors[1:]:
         below = below + f
-    att_scr[...] = above / below
+    for j in range(4):
+        above = jnp.zeros((32, 128), F32)
+        for p, f in zip(parts, factors):
+            above = above + f * p[32 * j : 32 * j + 32].astype(F32)
+        att_scr[:, 128 * j : 128 * j + 128] = above / below
     for i in range(8):
         for j in range(4):
             tile_scr[16 * i + 4 * j : 16 * i + 4 * j + 4, :] = att_scr[
@@ -567,39 +591,46 @@
     def gate_up(part):
         landed(xe.at[part].at[1:N_Y], p6b_r.at[part])
         rows = xe[part].reshape(64, COLS)
+        side = (core + part) % 2
+
+        def scatter(send, recv, ssem, rsem):
+            for dx in (2, 1, 3):
+                there = (x + dx) % 4
+                remote(
+                    send.at[part, there],
+                    recv.at[2 * dx + side - 1],
+                    ssem.at[part],
+                    rsem,
+                    there * 2 + part,
+                    ep,
+                ).start()
+
+            @pl.when(core != part)
+            def _():
+                remote(
+                    send.at[part, x], recv.at[0], ssem.at[part], rsem, x * 2 + part, ep
+                ).start()
+
+        p7_send[part] = dot(rows, gate_vm[...]).astype(BF16).reshape(N_Y, 16, HALF)
+        scatter(p7_send, p7_recv, p7_s, p7_r)
         rows32 = rows.astype(F32)
         squares = jnp.sum(rows32 * rows32, axis=1, keepdims=True)
-        p7_send[part, :, :, 2 * HALF :] = (
+        p7u_send[part, :, :, HALF:] = (
             three_parts(squares, (64, 128)).astype(BF16).reshape(N_Y, 16, 128)
         )
-        p7_send[part, :, :, :HALF] = dot(rows, gate_vm[...]).astype(BF16).reshape(N_Y, 16, HALF)
-        p7_send[part, :, :, HALF : 2 * HALF] = (
+        p7u_send[part, :, :, :HALF] = (
             dot(rows, up_vm[...]).astype(BF16).reshape(N_Y, 16, HALF)
         )
-        side = (core + part) % 2
-        for dx in (2, 1, 3):
-            there = (x + dx) % 4
-            remote(
-                p7_send.at[part, there],
-                p7_recv.at[2 * dx + side - 1],
-                p7_s.at[part],
-                p7_r,
-                there * 2 + part,
-                ep,
-            ).start()
+        scatter(p7u_send, p7u_recv, p7u_s, p7u_r)
+
+    def gate_up_sent(part):
+        for recv, sem in ((p7_recv, p7_s), (p7u_recv, p7u_s)):
+            landed(recv.at[0:3], sem.at[part])
 
         @pl.when(core != part)
         def _():
-            remote(
-                p7_send.at[part, x], p7_recv.at[0], p7_s.at[part], p7_r, x * 2 + part, ep
-            ).start()
-
-    def gate_up_sent(part):
-        landed(p7_recv.at[0:3], p7_s.at[part])
-
-        @pl.when(core != part)
-        def _():
-            landed(p7_recv.at[0], p7_s.at[part])
+            for recv, sem in ((p7_recv, p7_s), (p7u_recv, p7u_s)):
+                landed(recv.at[0], sem.at[part])
 
     landed(p6_recv.at[1:8], p6_r)
     pick_rows(0)
@@ -611,13 +642,17 @@
     pending.append(lambda: gate_up_sent(1))
 
     landed(p7_recv, p7_r)
-    sums = p7_send[core, x].astype(F32)
+    gate = p7_send[core, x].astype(F32)
     for i in range(N_CTX - 1):
-        sums = sums + p7_recv[i].astype(F32)
-    mean = jnp.sum(sums[:, 2 * HALF :], axis=1, keepdims=True) / D
+        gate = gate + p7_recv[i].astype(F32)
+    landed(p7u_recv, p7u_r)
+    sums = p7u_send[core, x].astype(F32)
+    for i in range(N_CTX - 1):
+        sums = sums + p7u_recv[i].astype(F32)
+    mean = jnp.sum(sums[:, HALF:], axis=1, keepdims=True) / D
     scale = lax.rsqrt(mean + epsilon)
-    gate = sums[:, :HALF] * scale
-    up = sums[:, HALF : 2 * HALF] * scale
+    gate = gate * scale
+    up = sums[:, :HALF] * scale
     middle = (gate / (1.0 + jnp.exp(-gate)) * up).astype(BF16)
     p8_send[...] = middle
     mid_all[core, x] = middle
@@ -720,8 +755,8 @@
         pltpu.VMEM((2, 2, 32, 128), BF16),
         pltpu.VMEM((4, 8, 128), F32),
         pltpu.VMEM((N_Z, 8, 128), F32),
-        pltpu.VMEM((N_CTX, 32, 640), BF16),
-        pltpu.VMEM((N_CTX - 1, 32, 640), BF16),
+        pltpu.VMEM((N_CTX, 144, 128), BF16),
+        pltpu.VMEM((N_CTX - 1, 144, 128), BF16),
         pltpu.VMEM((8, 16, 128), BF16),
         pltpu.VMEM((N_Z, 16, 128), BF16),
         pltpu.VMEM((64, 128), BF16),
@@ -732,8 +767,10 @@
         pltpu.VMEM((N_Z, 32, 128), BF16),
         pltpu.VMEM((2, N_Y, 16, COLS), BF16),
         pltpu.VMEM((2, N_Y, 16, COLS), BF16),
-        pltpu.VMEM((2, 4, 16, 1152), BF16),
-        pltpu.VMEM((N_CTX - 1, 16, 1152), BF16),
+        pltpu.VMEM((2, 4, 16, HALF), BF16),
+        pltpu.VMEM((N_CTX - 1, 16, HALF), BF16),
+        pltpu.VMEM((2, 4, 16, HALF + 128), BF16),
+        pltpu.VMEM((N_CTX - 1, 16, HALF + 128), BF16),
         pltpu.VMEM((16, HALF), BF16),
         pltpu.VMEM((2, 4, 16, HALF), BF16),
         pltpu.VMEM((2, N_Y, 16, COLS), BF16),
@@ -745,7 +782,7 @@
     scratch += [dma((3,)), dma]
     scratch += [dma((3,)), dma((3,))] + [dma] * 6 + [dma((7,)), dma] + [dma] * 6
     scratch += [dma((2,)), dma((2,))]
-    scratch += [dma((2,)), dma]
+    scratch += [dma((2,)), dma] * 2
     for count in (7, 2, 0):
         scratch += [dma((count,)), dma((count,))] if count else [dma, dma]
     both = pl.pallas_call(

time: 76.3 us -> 75.8 us (level)
  Pallas kernels: 74 us -> 73 us
    pallas_call x1, Pallas kernels: 74 us -> 73 us  [per_device(): pl.pallas_call(kernel, out_shape=jax.ShapeDtypeStruct((8, COLS), BF16), i...]
where the time goes in v6:
time: 75.8 us; the launch traced here: 75 us
  Pallas kernels  73 us (96%)
  local copies, waits for them, and re-layouts  1.39 us (2%)
    pallas_call x1, Pallas kernels, per_device(): pl.pallas_call(kernel, out_shape=jax.ShapeDtypeStruct((8, COLS), BF16), i...  73 us

profile of v6, /device:TPU:6, one launch (start us, length us, event | category | flops | bytes accessed | tf_op | source)
XLA Modules:
  0.0 75.0 jit_solution(7906258541261001923)
XLA Ops:
  0.6 73.0 %shard_map.149 = bf16[8,896]{1,0:T(8,128)(2,1)} custom-call(s32[4,1,4]{2,1,0:T(1,128)} %page_table_in.1, s32[4]{0:T(128)} %lengths_in.1, s32[4,8]{1,0:T(4,128)} %routes_in.1, f32[4,8]{1,0:T(4,128)} %route_weight_in.1, bf16[4,576]{1,0:T(4,128)(2,1)} %new_key_in.1, bf16[4,896]{1,0:T(4,128)(2,1)} %hidden_in.1, f32[896]{0:T(1024)} %gain_in.1, ...), custom_call_target="tpu_custom_call" | custom-call | tf_op jit(solution)/shard_map/pallas_call | solution.py:788
  73.6 1.4 %fusion = (bf16[4,896]{1,0:T(4,128)(2,1)}, bf16[4,896]{1,0:T(4,128)(2,1)}) fusion(bf16[8,896]{1,0:T(8,128)(2,1)} %shard_map.149), kind=kLoop, calls=%fused_computation | loop fusion | bytes 28672 | tf_op jit(solution)/shard_map/slice | solution.py:813

commit v7 on v6

--- a/solution.py
+++ b/solution.py
@@ -83,6 +83,7 @@
     wide_scr,
     z_scr,
     small_scr,
+    out_scr,
     hid_scr,
     gain_scr,
     res_scr,
@@ -569,7 +570,7 @@
     res_scr[...] = residual
     small_scr[...] = attention
     for j in range(NJ):
-        out[0:4, 128 * j : 128 * j + 128] = small_scr[4 * j : 4 * j + 4, :].astype(BF16)
+        out_scr[0:4, 128 * j : 128 * j + 128] = small_scr[4 * j : 4 * j + 4, :]
 
     def y_send(send, recv, ssem, rsem, sign):
         for k in y_order:
@@ -703,7 +704,8 @@
     landed(p10_recv, p10_s)
     small_scr[...] = res_scr[...] + routed
     for j in range(NJ):
-        out[4:8, 128 * j : 128 * j + 128] = small_scr[4 * j : 4 * j + 4, :].astype(BF16)
+        out_scr[4:8, 128 * j : 128 * j + 128] = small_scr[4 * j : 4 * j + 4, :]
+    out[...] = out_scr[...].astype(BF16)
 
 
 def per_device(
@@ -747,6 +749,7 @@
         pltpu.VMEM((64, COLS), F32),
         pltpu.VMEM((512, 128), F32),
         pltpu.VMEM((32, 128), F32),
+        pltpu.VMEM((8, COLS), F32),
         pltpu.VMEM((32, 128), F32),
         pltpu.VMEM((128, 128), F32),
         pltpu.VMEM((32, 128), F32),

time: 75.8 us -> 75.7 us (level)
  no operation moved by 1% of the time
where the time goes in v7:
time: 75.7 us; the launch traced here: 74.9 us
  Pallas kernels  72.8 us (96%)
  local copies, waits for them, and re-layouts  1.39 us (2%)
    pallas_call x1, Pallas kernels, per_device(): pl.pallas_call(kernel, out_shape=jax.ShapeDtypeStruct((8, COLS), BF16), i...  72.8 us

profile of v7, /device:TPU:6, one launch (start us, length us, event | category | flops | bytes accessed | tf_op | source)
XLA Modules:
  0.0 74.9 jit_solution(5539345235267280404)
XLA Ops:
  0.6 72.8 %shard_map.149 = bf16[8,896]{1,0:T(8,128)(2,1)} custom-call(s32[4,1,4]{2,1,0:T(1,128)} %page_table_in.1, s32[4]{0:T(128)} %lengths_in.1, s32[4,8]{1,0:T(4,128)} %routes_in.1, f32[4,8]{1,0:T(4,128)} %route_weight_in.1, bf16[4,576]{1,0:T(4,128)(2,1)} %new_key_in.1, bf16[4,896]{1,0:T(4,128)(2,1)} %hidden_in.1, f32[896]{0:T(1024)} %gain_in.1, ...), custom_call_target="tpu_custom_call" | custom-call | tf_op jit(solution)/shard_map/pallas_call | solution.py:791
  73.5 1.4 %fusion = (bf16[4,896]{1,0:T(4,128)(2,1)}, bf16[4,896]{1,0:T(4,128)(2,1)}) fusion(bf16[8,896]{1,0:T(8,128)(2,1)} %shard_map.149), kind=kLoop, calls=%fused_computation | loop fusion | bytes 28672 | tf_op jit(solution)/shard_map/slice | solution.py:816
